TPU v7x, 32 devices: a whole 2x2x4 slice. The times are simulated.
32 devices in a mesh: row: 4 (over z), col: 8 (over y, x, core).
Axes of the slice: x: 2, y: 2, z: 4, core: 2. Of those that a mesh axis runs over, the one named last changes fastest.
Arguments:
- tile_values: float32 [512, 512, 512], P(('row', 'col')), may hold values from -6 to 6
- tile_coords: int32 [512, 2], P(('row', 'col')), may hold values from 0 to 3, as said below
- tile_counts: int32 [32], P(('row', 'col')), may hold values from 4 to 16, as said below
- restrict_basis: float32 [8192, 256], P(('row', 'col')), may hold values from -0.25 to 0.25
- prolong_basis: float32 [16384, 256], P(('col', 'row')), may hold values from -0.25 to 0.25
- row_partner: int32 [8, 4], replicated, may hold values from 0 to 3, as said below
- col_partner: int32 [4, 8], replicated, may hold values from 0 to 7, as said below
Outputs:
- coarse: float32 [2048, 4096], P('row', 'col')
Inputs may be any that keep to these rules, and one draw needn't show every extreme that they name: `tile_coords`: within one device's 16 slots no two name the same (block row, block column); first entry below 4, second below 4; dead slots also hold such positions. `tile_counts`: number of leading slots of each device that are live; some device has all 16 live. `row_partner`: each row is a pairing: the partner of a part's partner is the part itself, never the part. `col_partner`: each row is a pairing: the partner of a part's partner is the part itself, never the part.
All inputs are finite; a program needn't handle non-finite values.
Results may differ from a plain program's by a relative error of at most 0.0003.
Values sent between devices are 32-bit elements; how exact they have to be, the bound alone decides.
No kernel may reach another device: no remote copies, remote signals or barrier semaphores. Data moves between devices by JAX's collectives and lax.ppermute only.
A program may use at most 128 MiB of HBM per device.

v0:
```python
import jax
import jax.numpy as jnp
from jax import lax
from jax.sharding import PartitionSpec as P


def pick_half(block, keep_flag, axis_dim):
    half_size = block.shape[axis_dim] // 2
    first = lax.slice_in_dim(block, 0, half_size, 1, axis_dim)
    second = lax.slice_in_dim(block, half_size, 2 * half_size, 1, axis_dim)
    kept = jnp.where(keep_flag, second, first)
    given = jnp.where(keep_flag, first, second)
    return (kept, given)


def body(
    tile_values, tile_coords, tile_counts, restrict_basis, prolong_basis, row_partner, col_partner
):
    restrict_part = lax.all_gather(restrict_basis, "col", axis=0, tiled=True)
    prolong_part = lax.all_gather(prolong_basis, "row", axis=0, tiled=True)
    tile_order = tile_values.shape[1]
    basis_width = restrict_basis.shape[1]
    block_rows = restrict_part.shape[0] // tile_order
    block_cols = prolong_part.shape[0] // tile_order
    live_count = tile_counts[0]

    def add_slot(slot_index, grid_now):
        block_row = tile_coords[slot_index, 0]
        block_col = tile_coords[slot_index, 1]
        left = lax.dynamic_slice_in_dim(restrict_part, block_row * tile_order, tile_order, 0)
        right = lax.dynamic_slice_in_dim(prolong_part, block_col * tile_order, tile_order, 0)
        applied = jnp.dot(tile_values[slot_index], right, precision=lax.Precision.HIGHEST)
        product = jnp.dot(left.T, applied, precision=lax.Precision.HIGHEST)
        product = jnp.where(slot_index < live_count, product, jnp.zeros_like(product))
        place = (block_row * basis_width, block_col * basis_width)
        current = lax.dynamic_slice(grid_now, place, (basis_width, basis_width))
        return lax.dynamic_update_slice(grid_now, current + product, place)

    start_grid = jnp.zeros((block_rows * basis_width, block_cols * basis_width), jnp.float32)
    local_grid = lax.fori_loop(0, tile_values.shape[0], add_slot, start_grid)
    my_row = lax.axis_index("row")
    my_col = lax.axis_index("col")
    row_table = row_partner[my_col]
    col_table = col_partner[my_row]
    partner_row = row_table[my_row]
    partner_col = col_table[my_col]
    keep_row = my_row > partner_row
    keep_col = my_col > partner_col
    kept, given = pick_half(local_grid, keep_row, 0)
    height = kept.shape[0]
    gathered = lax.all_gather(given, "row", axis=0, tiled=True)
    incoming = lax.dynamic_slice_in_dim(gathered, partner_row * height, height, 0)
    row_section = kept + incoming
    kept, given = pick_half(row_section, keep_col, 1)
    breadth = kept.shape[1]
    gathered = lax.all_gather(given, "col", axis=1, tiled=True)
    incoming = lax.dynamic_slice_in_dim(gathered, partner_col * breadth, breadth, 1)
    return kept + incoming


def solution(mesh):
    in_specs = (
        P(("row", "col"), None, None),
        P(("row", "col"), None),
        P(("row", "col")),
        P(("row", "col"), None),
        P(("col", "row"), None),
        P(),
        P(),
    )
    out_specs = P("row", "col")
    return jax.shard_map(body, mesh=mesh, in_specs=in_specs, out_specs=out_specs, check_vma=False)
```

profile of v0, /device:TPU:3, one launch (start us, length us, event | category | flops | bytes accessed | tf_op | source)
XLA Modules:
  0.0 454.6 jit_solution(13988054256300153918)
XLA Ops:
  10.1 46.0 %all-gather.7.cloned.1.call-done = f32[2048,256]{1,0:T(8,128)} async-done(((f32[512,256]{1,0:T(8,128)}), f32[2048,256]{1,0:T(8,128)}) %all-gather.7.cloned.1.call-update) | async-done | bytes 2097168 | tf_op jit(solution)/shard_map/all_gather | solution.py:20
  56.1 29.0 %all-gather.5.cloned.1.call-done = f32[2048,256]{1,0:T(8,128)} async-done(((f32[256,256]{1,0:T(8,128)}), f32[2048,256]{1,0:T(8,128)}) %all-gather.5.cloned.1.call-update) | async-done | bytes 2097168 | tf_op jit(solution)/shard_map/all_gather | solution.py:19
  85.1 2.5 broadcast_in_dim.3
  87.6 146.5 %while.13 = (s32[]{:T(128)}, f32[1024,1024]{1,0:T(8,128)}, s32[16,2]{0,1:T(2,128)S(1)}, s32[]{:T(128)}, f32[2048,256]{1,0:T(8,128)}, /*index=5*/f32[16,512,512]{...) while((s32[]{:T(128)}, f32[1024,1024]{1,0:T(8,128)}, ...), condition=%wide.region_1.2_spmd, body=%wide.region_0.1_spmd.sunk | while | flops 1208090624 | bytes 3670383 | solution.py:40
  93.9 2.9 fusion.21
  103.0 2.9 fusion.21
  109.8 2.4 fusion.20
  112.2 2.9 fusion.21
  121.4 2.9 fusion.21
  130.5 2.9 fusion.21
  139.7 2.9 fusion.21
  146.5 2.3 fusion.20
  148.8 2.9 fusion.21
  158.0 2.8 fusion.21
  167.2 2.9 fusion.21
  176.3 2.9 fusion.21
  183.1 2.3 fusion.20
  185.5 2.9 fusion.21
  192.3 2.4 fusion.20
  194.6 2.9 fusion.21
  201.5 2.3 fusion.20
  203.8 2.9 fusion.21
  210.6 2.4 fusion.20
  213.0 2.9 fusion.21
  219.8 2.3 fusion.20
  222.1 2.8 fusion.21
  231.3 2.9 fusion.21
  234.1 4.1 slice_select_fusion
  241.1 146.8 %all-gather.9.cloned.1.call-done = f32[2048,1024]{1,0:T(8,128)} async-done(((f32[512,1024]{1,0:T(8,128)}), f32[2048,1024]{1,0:T(8,128)}) %all-gather.9.cloned.1.call-update) | async-done | bytes 8388624 | tf_op jit(solution)/shard_map/all_gather | solution.py:51
  387.8 3.5 dynamic-slice_add_fusion
  393.3 52.3 %all-gather.11.cloned.1.call-done = f32[512,4096]{1,0:T(8,128)} async-done(((f32[512,512]{1,0:T(8,128)}), f32[512,4096]{1,0:T(8,128)}) %all-gather.11.cloned.1.call-update) | async-done | bytes 8388624 | tf_op jit(solution)/shard_map/all_gather | solution.py:56
  445.6 2.5 dynamic-slice_add_fusion.1
  (38 shorter events, 37.3 us)
Async XLA Ops:
  6.5 49.6 %all-gather.7.cloned.1.call-start = ((), (), s32[]{:S(2)}) async-start(), calls=%async_computation.1 | async-start | bytes 2621440 | tf_op jit(solution)/shard_map/all_gather | solution.py:20
  7.3 77.8 %all-gather.5.cloned.1.call-start = ((), (), s32[]{:S(2)}) async-start(), calls=%async_computation | async-start | bytes 2359296 | tf_op jit(solution)/shard_map/all_gather | solution.py:19
  8.0 379.8 %all-gather.9.cloned.1.call-start = ((), (), s32[]{:S(2)}) async-start(), calls=%async_computation.2 | async-start | bytes 10485760 | tf_op jit(solution)/shard_map/all_gather | solution.py:51
  85.1 2.5 copy-start
  238.3 207.3 %all-gather.11.cloned.1.call-start = ((), (), s32[]{:S(2)}) async-start(), calls=%async_computation.3 | async-start | bytes 9437184 | tf_op jit(solution)/shard_map/all_gather | solution.py:56
Sparse Core Ops, SparseCore 0:
  8.9 47.1 all-gather.6
  58.0 27.0 all-gather.4
  238.4 149.4 all-gather.8
  392.7 52.8 all-gather.10
where the time goes:
time: 457 us; the launch traced here: 455 us
  waiting for transfers between devices  275 us (60%)
  matrix products  83.4 us (18%)
  loops' own time  52.4 us (11%)
  local copies, waits for them, and re-layouts  16 us (4%)
  between operations  15.9 us (3%)
  other arithmetic  11.4 us (2%)
    all_gather x1, waiting for transfers between devices, body(): gathered = lax.all_gather(given, 'row', axis=0, tiled=True)  147 us
    another operation x1, loops' own time, body(): local_grid = lax.fori_loop(0, tile_values.shape[0], add_slot, start_grid)  52.4 us
    all_gather x1, waiting for transfers between devices, body(): gathered = lax.all_gather(given, 'col', axis=1, tiled=True)  52.3 us
    all_gather x1, waiting for transfers between devices, body(): prolong_part = lax.all_gather(prolong_basis, 'row', axis=0, tiled=True)  46 us
    dot_general x16, matrix products, add_slot(): product = jnp.dot(left.T, applied, precision=lax.Precision.HIGHEST)  45.8 us
    dot_general x16, matrix products, add_slot(): jnp.dot(tile_values[slot_index], right, precision=lax.Precision.HIGHEST)  37.6 us
    all_gather x1, waiting for transfers between devices, body(): restrict_part = lax.all_gather(restrict_basis, 'col', axis=0, tiled=True)  29 us
    dynamic_slice x16, local copies, waits for them, and re-layouts, add_slot(): block_col = tile_coords[slot_index, 1]  10.8 us
  transfers between devices with their start and end apart: 4, of which 4 were waited for; matrix products, arithmetic and copies ran while one was open for 1% of the time, Pallas kernels for 0%

commit v1 on v0

v1 whole, which is shorter than its diff:
```python
import jax
import jax.numpy as jnp
from jax import lax
from jax.experimental import pallas as pl
from jax.experimental.pallas import tpu as pltpu
from jax.sharding import PartitionSpec as P

F32 = jnp.float32
BF16 = jnp.bfloat16
VMEM_BYTES = 48 * 1024 * 1024


def split(value):
    high = value.astype(BF16)
    low = (value - high.astype(F32)).astype(BF16)
    return high, low


def dot(left, right):
    return jnp.dot(left, right, preferred_element_type=F32)


def product(left_high, left_low, right_high, right_low):
    return dot(left_high, right_high) + (dot(left_high, right_low) + dot(left_low, right_high))


def left_kernel(shards, block_cols, *refs):
    slot_ref, live_ref, place_ref = refs[:3]
    tile_ref = refs[3]
    pieces = refs[4 : 4 + shards]
    high_out, low_out, q_high, q_low = refs[4 + shards :]
    step = pl.program_id(0)
    tile_order = tile_ref.shape[1]
    depth = q_high.shape[2]
    per_block = tile_order // depth

    @pl.when(step == 0)
    def _():
        for index, piece in enumerate(pieces):
            high, low = split(piece[...])
            q_high[place_ref[index]] = high
            q_low[place_ref[index]] = low

    @pl.when(live_ref[step] == 1)
    def _():
        first = (step // block_cols) * per_block
        total = None
        for part in range(per_block):
            high, low = split(tile_ref[0, part * depth : (part + 1) * depth, :])
            term = product(q_high[first + part], q_low[first + part], high, low)
            total = term if total is None else total + term
        high, low = split(total)
        high_out[0] = high
        low_out[0] = low

    @pl.when(live_ref[step] == 0)
    def _():
        high_out[...] = jnp.zeros_like(high_out)
        low_out[...] = jnp.zeros_like(low_out)


def left_products(tiles, slots, live, pieces, places, block_cols):
    positions = slots.shape[0]
    tile_order = tiles.shape[1]
    width, depth = pieces[0].shape
    shards = len(pieces)
    whole = pl.BlockSpec((width, depth), lambda i, *_: (0, 0))
    out_spec = pl.BlockSpec((1, width, tile_order), lambda i, *_: (i, 0, 0))
    out = jax.ShapeDtypeStruct((positions, width, tile_order), BF16)
    return pl.pallas_call(
        lambda *refs: left_kernel(shards, block_cols, *refs),
        grid_spec=pltpu.PrefetchScalarGridSpec(
            num_scalar_prefetch=3,
            grid=(positions,),
            in_specs=[pl.BlockSpec((1, tile_order, tile_order), lambda i, s, *_: (s[i], 0, 0))]
            + [whole] * shards,
            out_specs=[out_spec, out_spec],
            scratch_shapes=[pltpu.VMEM((shards, width, depth), BF16)] * 2,
        ),
        out_shape=[out, out],
        compiler_params=pltpu.CompilerParams(vmem_limit_bytes=VMEM_BYTES),
        cost_estimate=pl.CostEstimate(
            flops=6 * positions * width * tile_order * tile_order,
            bytes_accessed=4 * tiles.size + 4 * positions * width * tile_order,
            transcendentals=0,
        ),
        name="left_products",
    )(slots, live, places, tiles, *pieces)


def right_kernel(shards, chunks, per_chunk, *refs):
    place_ref, column_ref, shard_ref = refs[:3]
    high_ref, low_ref = refs[3:5]
    pieces = refs[5 : 5 + shards]
    outs = refs[5 + shards : 5 + shards + chunks]
    p_high, p_low = refs[5 + shards + chunks :]
    step = pl.program_id(0)
    tile_order = high_ref.shape[2]
    depth = pieces[0].shape[0]

    @pl.when(step == 0)
    def _():
        for index, piece in enumerate(pieces):

            @pl.when(shard_ref[index] >= 0)
            def _():
                high, low = split(piece[...])
                rows = pl.ds(pl.multiple_of(shard_ref[index] * depth, depth), depth)
                p_high[rows, :] = high
                p_low[rows, :] = low

    chunk = step // per_chunk
    start = pl.multiple_of(column_ref[chunk] * tile_order, tile_order)
    rows = pl.ds(start, tile_order)
    block = product(high_ref[0], low_ref[0], p_high[rows, :], p_low[rows, :])
    for index in range(chunks):

        @pl.when(chunk == index)
        def _():
            outs[index][...] = block


def right_products(w_high, w_low, positions, columns, pieces, shard_of, shard_count):
    steps = positions.shape[0]
    chunks = columns.shape[0]
    per_chunk = steps // chunks
    _, width, tile_order = w_high.shape
    depth, _ = pieces[0].shape
    shards = len(pieces)
    w_spec = pl.BlockSpec((1, width, tile_order), lambda i, pos, *_: (pos[i], 0, 0))
    whole = pl.BlockSpec((depth, width), lambda i, *_: (0, 0))

    def out_spec(index):
        first = index * per_chunk
        return pl.BlockSpec(
            (width, width), lambda i, *_: (jnp.clip(i - first, 0, per_chunk - 1), 0)
        )

    return pl.pallas_call(
        lambda *refs: right_kernel(shards, chunks, per_chunk, *refs),
        grid_spec=pltpu.PrefetchScalarGridSpec(
            num_scalar_prefetch=3,
            grid=(steps,),
            in_specs=[w_spec, w_spec] + [whole] * shards,
            out_specs=[out_spec(index) for index in range(chunks)],
            scratch_shapes=[pltpu.VMEM((shard_count * depth, width), BF16)] * 2,
        ),
        out_shape=[jax.ShapeDtypeStruct((per_chunk * width, width), F32)] * chunks,
        compiler_params=pltpu.CompilerParams(vmem_limit_bytes=VMEM_BYTES),
        cost_estimate=pl.CostEstimate(
            flops=6 * steps * width * width * tile_order,
            bytes_accessed=4 * steps * width * (tile_order + width),
            transcendentals=0,
        ),
        name="right_products",
    )(positions, columns, shard_of, w_high, w_low, *pieces)


def flip(value, axis, size, mask):
    return lax.ppermute(value, axis, [(i, i ^ mask) for i in range(size)])


def gather_restrict(shard, axis, size, me):
    if size == 8:
        pieces = [shard] + [flip(shard, axis, size, mask) for mask in range(1, size)]
        places = me ^ jnp.arange(size, dtype=jnp.int32)
        return pieces, places
    gathered = lax.all_gather(shard, axis)
    return [gathered[i] for i in range(size)], jnp.arange(size, dtype=jnp.int32)


def gather_prolong(shard, axis, size, me):
    if size != 4:
        gathered = lax.all_gather(shard, axis)
        return [gathered[i] for i in range(size)], jnp.arange(size, dtype=jnp.int32)
    pieces, shard_of = [shard], [me]
    up = down = shard
    for step in range(1, size):
        up = lax.ppermute(up, axis, [(i, i + 1) for i in range(step - 1, size - 1)])
        down = lax.ppermute(down, axis, [(i + 1, i) for i in range(size - step)])
        pieces += [up, down]
        shard_of += [me - step, jnp.where(me + step < size, me + step, -1)]
    return pieces, jnp.stack(shard_of).astype(jnp.int32)


def row_exchange(chunk, axis, size, kind, me, partner):
    if size != 4:
        gathered = lax.all_gather(chunk, axis)
        return lax.dynamic_index_in_dim(gathered, partner, 0, keepdims=False)
    outer = lax.ppermute(chunk, axis, [(0, 1), (3, 2)])
    own_over = lax.ppermute(chunk, axis, [(1, 2), (2, 1)])
    outer_over = lax.ppermute(outer, axis, [(1, 2), (2, 1)])
    handed = jnp.where(kind == 1, chunk, jnp.where(kind == 2, own_over, outer_over))
    handed = lax.ppermute(handed, axis, [(1, 0), (2, 3)])
    inner = jnp.where(kind == 1, outer, jnp.where(kind == 2, outer_over, own_over))
    return jnp.where((me == 1) | (me == 2), inner, handed)


def col_exchange(chunk, axis, size, me, partner, mate_partner, turn):
    if size != 8:
        gathered = lax.all_gather(chunk, axis)
        return lax.dynamic_index_in_dim(gathered, partner, 0, keepdims=False)
    over_x = flip(chunk, axis, size, 2)
    over_y = flip(chunk, axis, size, 4)
    over_both = flip(over_y, axis, size, 2) if turn else flip(over_x, axis, size, 4)

    def pick(chip):
        return jnp.where(
            chip == 0, chunk, jnp.where(chip == 2, over_x, jnp.where(chip == 4, over_y, over_both))
        )

    from_mate = flip(pick((me ^ 1 ^ mate_partner) & 6), axis, size, 1)
    mine = me ^ partner
    return jnp.where((mine & 1) == 1, from_mate, pick(mine & 6))


def solution(mesh):
    n_row = mesh.shape["row"]
    n_col = mesh.shape["col"]

    def body(tiles, coords, counts, restrict, prolong, row_partner, col_partner):
        slot_count, tile_order, _ = tiles.shape
        block_rows = restrict.shape[0] * n_col // tile_order
        block_cols = prolong.shape[0] * n_row // tile_order
        positions = jnp.arange(block_rows * block_cols, dtype=jnp.int32)
        row = lax.axis_index("row").astype(jnp.int32)
        col = lax.axis_index("col").astype(jnp.int32)

        q_pieces, q_places = gather_restrict(restrict.T, "col", n_col, col)
        p_pieces, p_shards = gather_prolong(prolong, "row", n_row, row)

        slot_ids = jnp.arange(slot_count, dtype=jnp.int32)
        hits = (coords[:, 0] * block_cols + coords[:, 1])[None, :] == positions[:, None]
        live = jnp.any(hits & (slot_ids < counts[0])[None, :], axis=1).astype(jnp.int32)
        slots = jnp.sum(jnp.where(hits, slot_ids[None, :], 0), axis=1).astype(jnp.int32)

        row_mate = row_partner[col, row]
        col_mate = col_partner[row, col]
        keep_row = (row > row_mate).astype(jnp.int32)
        keep_col = (col > col_mate).astype(jnp.int32)
        mate_keep_col = (col > col_partner[row_mate, col]).astype(jnp.int32)
        half_rows = block_rows // 2
        half_cols = block_cols // 2

        def order(row_half, col_half):
            ids = jnp.arange(block_cols, dtype=jnp.int32)
            columns = (ids + (1 - col_half) * half_cols) % block_cols
            rows = jnp.arange(half_rows, dtype=jnp.int32) + row_half * half_rows
            places = rows[None, :] * block_cols + columns[:, None]
            return places.reshape(-1).astype(jnp.int32), columns.astype(jnp.int32)

        w_high, w_low = left_products(tiles, slots, live, q_pieces, q_places, block_cols)
        places, columns = order(1 - keep_row, mate_keep_col)
        given = right_products(w_high, w_low, places, columns, p_pieces, p_shards, n_row)
        places, columns = order(keep_row, keep_col)
        kept = right_products(w_high, w_low, places, columns, p_pieces, p_shards, n_row)

        kind = row ^ row_mate
        sums = [
            own + row_exchange(chunk, "row", n_row, kind, row, row_mate)
            for own, chunk in zip(kept, given)
        ]
        mate_partner = col_partner[row, col ^ 1]
        quarters = [
            sums[half_cols + i]
            + col_exchange(sums[i], "col", n_col, col, col_mate, mate_partner, i % 2)
            for i in range(half_cols)
        ]
        return jnp.concatenate(quarters, axis=1)

    in_specs = (
        P(("row", "col"), None, None),
        P(("row", "col"), None),
        P(("row", "col")),
        P(("row", "col"), None),
        P(("col", "row"), None),
        P(),
        P(),
    )
    return jax.shard_map(
        body, mesh=mesh, in_specs=in_specs, out_specs=P("row", "col"), check_vma=False
    )
```

time: 457 us -> 215 us (0.47)
  waiting for transfers between devices: 275 us -> 57.3 us
  matrix products: 83.4 us -> 0 us
  starting transfers between devices: 0.12 us -> 79.7 us
  loops' own time: 52.4 us -> 0 us
  Pallas kernels: 0 us -> 35.2 us
  between operations: 15.9 us -> 7.15 us
  other arithmetic: 11.4 us -> 17.8 us
    all_gather x4 -> x0, waiting for transfers between devices: 274 us -> none  [the longest x1 147 us: body(): gathered = lax.all_gather(given, 'row', axis=0, tiled=True)]
    dot_general x32 -> x0, matrix products: 83.4 us -> none  [the longest x16 45.8 us: add_slot(): product = jnp.dot(left.T, applied, precision=lax.Precision.HIGHEST)]
    ppermute x0 -> x37, starting transfers between devices: none -> 79.7 us  [the longest x4 33.4 us: row_exchange(): outer = lax.ppermute(chunk, axis, [(0, 1), (3, 2)])]
    ppermute x0 -> x37, waiting for transfers between devices: none -> 57.3 us  [the longest x15 30.1 us: flip(): return lax.ppermute(value, axis, [(i, i ^ mask) for i in range(size)])]
    another operation x1 -> x0, loops' own time: 52.4 us -> none  [body(): local_grid = lax.fori_loop(0, tile_values.shape[0], add_slot, start_grid)]
    pallas_call x0 -> x3, Pallas kernels: none -> 35.2 us  [the longest x1 19.2 us: left_products(): pl.pallas_call(lambda *refs: left_kernel(shards, block_cols, *refs), grid...]
    unnamed x2 -> x59, local copies, waits for them, and re-layouts: 0.01 us -> 11.3 us
    dynamic_slice x18 -> x2, local copies, waits for them, and re-layouts: 13.5 us -> 2.81 us  [the longest x1 1.45 us: body(): mate_partner = col_partner[row, col ^ 1]]
  transfers between devices with their start and end apart: 4 -> 37, of which waited for: 4 -> 11; matrix products, arithmetic and copies ran while one was open for 1% -> 8% of each run, Pallas kernels for 0% -> 13%
where the time goes in v1:
time: 215 us; the launch traced here: 212 us
  starting transfers between devices  79.7 us (37%)
  waiting for transfers between devices  57.3 us (27%)
  Pallas kernels  35.2 us (16%)
  other arithmetic  17.8 us (8%)
  local copies, waits for them, and re-layouts  14.4 us (7%)
  between operations  7.15 us (3%)
    ppermute x4, starting transfers between devices, row_exchange(): outer = lax.ppermute(chunk, axis, [(0, 1), (3, 2)])  33.4 us
    ppermute x15, waiting for transfers between devices, flip(): return lax.ppermute(value, axis, [(i, i ^ mask) for i in range(size)])  30.1 us
    ppermute x15, starting transfers between devices, flip(): return lax.ppermute(value, axis, [(i, i ^ mask) for i in range(size)])  23.7 us
    pallas_call x1, Pallas kernels, left_products(): pl.pallas_call(lambda *refs: left_kernel(shards, block_cols, *refs), grid...  19.2 us
    pallas_call x2, Pallas kernels, right_products(): pl.pallas_call(lambda *refs: right_kernel(shards, chunks, per_chunk, *ref...  15.9 us
    ppermute x4, waiting for transfers between devices, row_exchange(): outer = lax.ppermute(chunk, axis, [(0, 1), (3, 2)])  15.4 us
    unnamed x59, local copies, waits for them, and re-layouts  11.3 us
    ppermute x3, waiting for transfers between devices, gather_prolong(): down = lax.ppermute(down, axis, [(i + 1, i) for i in range(size - step)])  7.85 us
  transfers between devices with their start and end apart: 37, of which 11 were waited for; matrix products, arithmetic and copies ran while one was open for 8% of the time, Pallas kernels for 13%

profile of v1, /device:TPU:3, one launch (start us, length us, event | category | flops | bytes accessed | tf_op | source)
XLA Modules:
  0.0 211.6 jit_solution(9024264510285530903)
XLA Ops:
  1.8 1.7 collective-permute-start.2
  3.5 3.2 %collective-permute-start.7 = (f32[512,256]{1,0:T(8,128)}, f32[512,256]{1,0:T(8,128)S(1)}, u32[]{:S(2)}, u32[]{:S(2)}) collective-permute-start(f32[512,256]{1,0:T(8,128)} %refs_5_.3), channel_id=1, source_target_pairs={{0,8},{8,16},{16,24},{1,9},{9,17},{17,25},{2,10},{10,18},{18,26},{... | collective-permute-start | bytes 1572872 | tf_op jit(solution)/shard_map/ppermute | solution.py:179
  18.9 3.0 %collective-permute-done.8.refs_7_ = f32[512,256]{1,0:T(8,128)S(1)} collective-permute-done((f32[512,256]{1,0:T(8,128)}, f32[512,256]{1,0:T(8,128)S(1)}, u32[]{:S(2)}, u32[]{:S(2)}) %collective-permute-start.8) | collective-permute-done | bytes 524320 | tf_op jit(solution)/shard_map/ppermute | solution.py:180
  24.7 2.4 %collective-permute-start.4 = (f32[256,256]{1,0:T(8,128)S(1)}, f32[256,256]{1,0:T(8,128)}, u32[]{:S(2)}, u32[]{:S(2)}) collective-permute-start(f32[256,256]{1,0:T(8,128)S(1)} %bitcast.20), channel_id=1, source_target_pairs={{0,5},{1,4},{2,7},{3,6},{4,1},{5,0},{6,3},{7,2},{8,13},{9,12},{10,... | collective-permute-start | bytes 786440 | tf_op jit(solution)/shard_map/ppermute | solution.py:160
  28.7 1.6 collective-permute-start.6
  31.6 4.8 %collective-permute-done.10.refs_9_ = f32[512,256]{1,0:T(8,128)S(1)} collective-permute-done((f32[512,256]{1,0:T(8,128)S(1)}, f32[512,256]{1,0:T(8,128)S(1)}, u32[]{:S(2)}, u32[]{:S(2)}) %collective-permute-start.10) | collective-permute-done | bytes 524320 | tf_op jit(solution)/shard_map/ppermute | solution.py:180
  37.7 7.8 %collective-permute-done.4.refs_9_ = f32[256,256]{1,0:T(8,128)} collective-permute-done((f32[256,256]{1,0:T(8,128)S(1)}, f32[256,256]{1,0:T(8,128)}, u32[]{:S(2)}, u32[]{:S(2)}) %collective-permute-start.4) | collective-permute-done | bytes 262176 | tf_op jit(solution)/shard_map/ppermute | solution.py:160
  49.3 19.2 %left_products.1 = (bf16[16,256,512]{2,1,0:T(8,128)(2,1)}, bf16[16,256,512]{2,1,0:T(8,128)(2,1)}) custom-call(s32[16]{0:T(128)S(1)} %select_reduce_fusion.refs_0_, s32[16]{0:T(128)S(1)} %convert_element_type.13.refs_1_, s32[8]{0:T(128)S(1)} %iota_xor_fusion.refs_2_, f32[16,512,512]{2,1,0:T(8,128)} %refs_3_.1, f32[256,256]{1,0:T(8,128)S(1)} %bitcast.23, ...), custom_call_target="tpu_custom_call" | custom-call | flops 6442450944 | bytes 25165824 | tf_op jit(solution)/shard_map/left_products/pallas_call | solution.py:70
  68.5 8.6 %right_products.3 = (f32[512,256]{1,0:T(8,128)}, f32[512,256]{1,0:T(8,128)}, f32[512,256]{1,0:T(8,128)}, f32[512,256]{1,0:T(8,128)S(1)}) custom-call(s32[8]{0:T(128)S(1)} %add.176.refs_0_, s32[4]{0:T(128)S(1)} %and_select_fusion.refs_1_, s32[7]{0:T(128)S(1)} %stack.31.refs_2_, bf16[16,256,512]{2,1,0:T(8,128)(2,1)} %get-tuple-element.15.refs_3_, ...), custom_call_target="tpu_custom_call" | custom-call | flops 1610612736 | bytes 6291456 | tf_op jit(solution)/shard_map/right_products/pallas_call | solution.py:139
  78.0 5.1 %collective-permute-start.29 = (f32[512,256]{1,0:T(8,128)}, f32[512,256]{1,0:T(8,128)}, u32[]{:S(2)}, u32[]{:S(2)}) collective-permute-start(f32[512,256]{1,0:T(8,128)} %get-tuple-element.24), channel_id=1, source_target_pairs={{0,8},{24,16},{1,9},{25,17},{2,10},{26,18},{3,11},{27,19},{4,12},{... | collective-permute-start | bytes 1572872 | tf_op jit(solution)/shard_map/ppermute | solution.py:190
  83.1 2.1 collective-permute-start.17
  85.2 1.5 collective-permute-start.31
  86.7 7.7 %collective-permute-done.29 = f32[512,256]{1,0:T(8,128)} collective-permute-done((f32[512,256]{1,0:T(8,128)}, f32[512,256]{1,0:T(8,128)}, u32[]{:S(2)}, u32[]{:S(2)}) %collective-permute-start.29) | collective-permute-done | bytes 524320 | tf_op jit(solution)/shard_map/ppermute | solution.py:190
  97.9 6.0 %collective-permute-done.17 = f32[512,256]{1,0:T(8,128)} collective-permute-done((f32[512,256]{1,0:T(8,128)}, f32[512,256]{1,0:T(8,128)}, u32[]{:S(2)}, u32[]{:S(2)}) %collective-permute-start.17) | collective-permute-done | bytes 524320 | tf_op jit(solution)/shard_map/ppermute | solution.py:190
  106.1 2.0 select_select_fusion.1
  110.3 10.0 %collective-permute-start.25 = (f32[512,256]{1,0:T(8,128)}, f32[512,256]{1,0:T(8,128)}, u32[]{:S(2)}, u32[]{:S(2)}) collective-permute-start(f32[512,256]{1,0:T(8,128)} %copy-done.7), channel_id=1, source_target_pairs={{0,8},{24,16},{1,9},{25,17},{2,10},{26,18},{3,11},{27,19},{4,12},{... | collective-permute-start | bytes 1572872 | tf_op jit(solution)/shard_map/ppermute | solution.py:190
  123.8 7.3 %right_products.2 = (f32[512,256]{1,0:T(8,128)S(1)}, f32[512,256]{1,0:T(8,128)S(1)}, f32[512,256]{1,0:T(8,128)S(1)}, f32[512,256]{1,0:T(8,128)S(1)}) custom-call(s32[8]{0:T(128)S(1)} %add.161.refs_0_, s32[4]{0:T(128)S(1)} %and_select_fusion.1.refs_1_, s32[7]{0:T(128)S(1)} %stack.31.refs_2_, bf16[16,256,512]{2,1,0:T(8,128)(2,1)} %get-tuple-element.15.refs_3_, ...), custom_call_target="tpu_custom_call" | custom-call | flops 1610612736 | bytes 6291456 | tf_op jit(solution)/shard_map/right_products/pallas_call | solution.py:139
  134.2 16.2 %collective-permute-start.13 = (f32[512,256]{1,0:T(8,128)}, f32[512,256]{1,0:T(8,128)}, u32[]{:S(2)}, u32[]{:S(2)}) collective-permute-start(f32[512,256]{1,0:T(8,128)} %get-tuple-element.18), channel_id=1, source_target_pairs={{0,8},{24,16},{1,9},{25,17},{2,10},{26,18},{3,11},{27,19},{4,12},{... | collective-permute-start | bytes 1572872 | tf_op jit(solution)/shard_map/ppermute | solution.py:190
  152.5 1.7 collective-permute-start.21
  155.4 1.7 collective-permute-done.13
  158.6 1.9 select_select_fusion.2
  162.0 9.6 %collective-permute-done.21 = f32[512,256]{1,0:T(8,128)} collective-permute-done((f32[512,256]{1,0:T(8,128)S(1)}, f32[512,256]{1,0:T(8,128)}, u32[]{:S(2)}, u32[]{:S(2)}) %collective-permute-start.21) | collective-permute-done | bytes 524320 | tf_op jit(solution)/shard_map/ppermute | solution.py:160
  171.7 2.2 %collective-permute-start.22 = (f32[512,256]{1,0:T(8,128)S(1)}, f32[512,256]{1,0:T(8,128)S(1)}, u32[]{:S(2)}, u32[]{:S(2)}) collective-permute-start(f32[512,256]{1,0:T(8,128)S(1)} %select_add_fusion.3), channel_id=1, source_target_pairs={{0,4},{1,5},{2,6},{3,7},{4,0},{5,1},{6,2},{7,3},{8,12},{9,13},{10,... | collective-permute-start | bytes 1572872 | tf_op jit(solution)/shard_map/ppermute | solution.py:160
  173.9 9.1 %collective-permute-done.35 = f32[512,256]{1,0:T(8,128)} collective-permute-done((f32[512,256]{1,0:T(8,128)S(1)}, f32[512,256]{1,0:T(8,128)}, u32[]{:S(2)}, u32[]{:S(2)}) %collective-permute-start.35) | collective-permute-done | bytes 524320 | tf_op jit(solution)/shard_map/ppermute | solution.py:160
  182.9 2.2 %collective-permute-start.23 = (f32[512,256]{1,0:T(8,128)}, f32[512,256]{1,0:T(8,128)S(1)}, u32[]{:S(2)}, u32[]{:S(2)}) collective-permute-start(f32[512,256]{1,0:T(8,128)} %collective-permute-done.21), channel_id=1, source_target_pairs={{0,4},{1,5},{2,6},{3,7},{4,0},{5,1},{6,2},{7,3},{8,12},{9,13},{10,... | collective-permute-start | bytes 1572872 | tf_op jit(solution)/shard_map/ppermute | solution.py:160
  185.1 2.0 select_select_fusion
  187.1 4.7 %collective-permute-start.36 = (f32[512,256]{1,0:T(8,128)}, f32[512,256]{1,0:T(8,128)}, u32[]{:S(2)}, u32[]{:S(2)}) collective-permute-start(f32[512,256]{1,0:T(8,128)} %select_select_fusion), channel_id=1, source_target_pairs={{0,1},{1,0},{2,3},{3,2},{4,5},{5,4},{6,7},{7,6},{8,9},{9,8},{10,11... | collective-permute-start | bytes 1572872 | tf_op jit(solution)/shard_map/ppermute | solution.py:160
  194.3 3.6 %collective-permute-done.23 = f32[512,256]{1,0:T(8,128)S(1)} collective-permute-done((f32[512,256]{1,0:T(8,128)}, f32[512,256]{1,0:T(8,128)S(1)}, u32[]{:S(2)}, u32[]{:S(2)}) %collective-permute-start.23) | collective-permute-done | bytes 524320 | tf_op jit(solution)/shard_map/ppermute | solution.py:160
  198.8 4.3 %collective-permute-start.24 = (f32[512,256]{1,0:T(8,128)}, f32[512,256]{1,0:T(8,128)}, u32[]{:S(2)}, u32[]{:S(2)}) collective-permute-start(f32[512,256]{1,0:T(8,128)} %select_select_fusion.3), channel_id=1, source_target_pairs={{0,1},{1,0},{2,3},{3,2},{4,5},{5,4},{6,7},{7,6},{8,9},{9,8},{10,11... | collective-permute-start | bytes 1572872 | tf_op jit(solution)/shard_map/ppermute | solution.py:160
  203.8 2.0 select_add_fusion
  205.8 2.8 %collective-permute-done.16 = f32[512,256]{1,0:T(8,128)} collective-permute-done((f32[512,256]{1,0:T(8,128)}, f32[512,256]{1,0:T(8,128)}, u32[]{:S(2)}, u32[]{:S(2)}) %collective-permute-start.16) | collective-permute-done | bytes 524320 | tf_op jit(solution)/shard_map/ppermute | solution.py:194
  208.7 1.8 select_add_fusion.2
  (132 shorter events, 44.7 us)
Async XLA Ops:
  1.1 14.0 %collective-permute-start = (f32[256,256]{1,0:T(8,128)S(1)}, f32[256,256]{1,0:T(8,128)S(1)}, u32[]{:S(2)}, u32[]{:S(2)}) collective-permute-start(f32[256,256]{1,0:T(8,128)S(1)} %bitcast.16), channel_id=1, source_target_pairs={{0,1},{1,0},{2,3},{3,2},{4,5},{5,4},{6,7},{7,6},{8,9},{9,8},{10,11... | collective-permute-start | bytes 786440 | tf_op jit(solution)/shard_map/ppermute | solution.py:160
  1.8 22.2 %collective-permute-start.1 = (f32[256,256]{1,0:T(8,128)S(1)}, f32[256,256]{1,0:T(8,128)S(1)}, u32[]{:S(2)}, u32[]{:S(2)}) collective-permute-start(f32[256,256]{1,0:T(8,128)S(1)} %bitcast.17), channel_id=1, source_target_pairs={{0,2},{1,3},{2,0},{3,1},{4,6},{5,7},{6,4},{7,5},{8,10},{9,11},{10,... | collective-permute-start | bytes 786440 | tf_op jit(solution)/shard_map/ppermute | solution.py:160
  1.8 25.3 %collective-permute-start.2 = (f32[256,256]{1,0:T(8,128)S(1)}, f32[256,256]{1,0:T(8,128)S(1)}, u32[]{:S(2)}, u32[]{:S(2)}) collective-permute-start(f32[256,256]{1,0:T(8,128)S(1)} %bitcast.18), channel_id=1, source_target_pairs={{0,3},{1,2},{2,1},{3,0},{4,7},{5,6},{6,5},{7,4},{8,11},{9,10},{10,... | collective-permute-start | bytes 786440 | tf_op jit(solution)/shard_map/ppermute | solution.py:160
  3.5 14.7 %collective-permute-start.7 = (f32[512,256]{1,0:T(8,128)}, f32[512,256]{1,0:T(8,128)S(1)}, u32[]{:S(2)}, u32[]{:S(2)}) collective-permute-start(f32[512,256]{1,0:T(8,128)} %refs_5_.3), channel_id=1, source_target_pairs={{0,8},{8,16},{16,24},{1,9},{9,17},{17,25},{2,10},{10,18},{18,26},{... | collective-permute-start | bytes 1572872 | tf_op jit(solution)/shard_map/ppermute | solution.py:179
  6.8 15.2 %collective-permute-start.8 = (f32[512,256]{1,0:T(8,128)}, f32[512,256]{1,0:T(8,128)S(1)}, u32[]{:S(2)}, u32[]{:S(2)}) collective-permute-start(f32[512,256]{1,0:T(8,128)} %refs_5_.3), channel_id=1, source_target_pairs={{8,0},{16,8},{24,16},{9,1},{17,9},{25,17},{10,2},{18,10},{26,18},{... | collective-permute-start | bytes 1572872 | tf_op jit(solution)/shard_map/ppermute | solution.py:180
  18.2 12.5 %collective-permute-start.9 = (f32[512,256]{1,0:T(8,128)S(1)}, f32[512,256]{1,0:T(8,128)S(1)}, u32[]{:S(2)}, u32[]{:S(2)}) collective-permute-start(f32[512,256]{1,0:T(8,128)S(1)} %collective-permute-done.7.refs_6_), channel_id=1, source_target_pairs={{8,16},{16,24},{9,17},{17,25},{10,18},{18,26},{11,19},{19,27},{12,... | collective-permute-start | bytes 1572872 | tf_op jit(solution)/shard_map/ppermute | solution.py:179
  21.9 14.5 %collective-permute-start.10 = (f32[512,256]{1,0:T(8,128)S(1)}, f32[512,256]{1,0:T(8,128)S(1)}, u32[]{:S(2)}, u32[]{:S(2)}) collective-permute-start(f32[512,256]{1,0:T(8,128)S(1)} %collective-permute-done.8.refs_7_), channel_id=1, source_target_pairs={{8,0},{16,8},{9,1},{17,9},{10,2},{18,10},{11,3},{19,11},{12,4},{20... | collective-permute-start | bytes 1572872 | tf_op jit(solution)/shard_map/ppermute | solution.py:180
  24.7 20.8 %collective-permute-start.4 = (f32[256,256]{1,0:T(8,128)S(1)}, f32[256,256]{1,0:T(8,128)}, u32[]{:S(2)}, u32[]{:S(2)}) collective-permute-start(f32[256,256]{1,0:T(8,128)S(1)} %bitcast.20), channel_id=1, source_target_pairs={{0,5},{1,4},{2,7},{3,6},{4,1},{5,0},{6,3},{7,2},{8,13},{9,12},{10,... | collective-permute-start | bytes 786440 | tf_op jit(solution)/shard_map/ppermute | solution.py:160
  27.8 17.6 %collective-permute-start.5 = (f32[256,256]{1,0:T(8,128)S(1)}, f32[256,256]{1,0:T(8,128)}, u32[]{:S(2)}, u32[]{:S(2)}) collective-permute-start(f32[256,256]{1,0:T(8,128)S(1)} %bitcast.21), channel_id=1, source_target_pairs={{0,6},{1,7},{2,4},{3,5},{4,2},{5,3},{6,0},{7,1},{8,14},{9,15},{10,... | collective-permute-start | bytes 786440 | tf_op jit(solution)/shard_map/ppermute | solution.py:160
  28.7 16.7 %collective-permute-start.6 = (f32[256,256]{1,0:T(8,128)S(1)}, f32[256,256]{1,0:T(8,128)}, u32[]{:S(2)}, u32[]{:S(2)}) collective-permute-start(f32[256,256]{1,0:T(8,128)S(1)} %bitcast.22), channel_id=1, source_target_pairs={{0,7},{1,6},{2,5},{3,4},{4,3},{5,2},{6,1},{7,0},{8,15},{9,14},{10,... | collective-permute-start | bytes 786440 | tf_op jit(solution)/shard_map/ppermute | solution.py:160
  30.7 37.8 %collective-permute-start.11 = (f32[512,256]{1,0:T(8,128)S(1)}, f32[512,256]{1,0:T(8,128)S(1)}, u32[]{:S(2)}, u32[]{:S(2)}) collective-permute-start(f32[512,256]{1,0:T(8,128)S(1)} %collective-permute-done.9.refs_8_), channel_id=1, source_target_pairs={{16,24},{17,25},{18,26},{19,27},{20,28},{21,29},{22,30},{23,31}} | collective-permute-start | bytes 1572872 | tf_op jit(solution)/shard_map/ppermute | solution.py:179
  36.4 32.1 %collective-permute-start.12 = (f32[512,256]{1,0:T(8,128)S(1)}, f32[512,256]{1,0:T(8,128)S(1)}, u32[]{:S(2)}, u32[]{:S(2)}) collective-permute-start(f32[512,256]{1,0:T(8,128)S(1)} %collective-permute-done.10.refs_9_), channel_id=1, source_target_pairs={{8,0},{9,1},{10,2},{11,3},{12,4},{13,5},{14,6},{15,7}} | collective-permute-start | bytes 1572872 | tf_op jit(solution)/shard_map/ppermute | solution.py:180
  78.0 16.4 %collective-permute-start.29 = (f32[512,256]{1,0:T(8,128)}, f32[512,256]{1,0:T(8,128)}, u32[]{:S(2)}, u32[]{:S(2)}) collective-permute-start(f32[512,256]{1,0:T(8,128)} %get-tuple-element.24), channel_id=1, source_target_pairs={{0,8},{24,16},{1,9},{25,17},{2,10},{26,18},{3,11},{27,19},{4,12},{... | collective-permute-start | bytes 1572872 | tf_op jit(solution)/shard_map/ppermute | solution.py:190
  83.1 20.8 %collective-permute-start.17 = (f32[512,256]{1,0:T(8,128)}, f32[512,256]{1,0:T(8,128)}, u32[]{:S(2)}, u32[]{:S(2)}) collective-permute-start(f32[512,256]{1,0:T(8,128)} %get-tuple-element.20), channel_id=1, source_target_pairs={{0,8},{24,16},{1,9},{25,17},{2,10},{26,18},{3,11},{27,19},{4,12},{... | collective-permute-start | bytes 1572872 | tf_op jit(solution)/shard_map/ppermute | solution.py:190
  85.2 20.9 %collective-permute-start.31 = (f32[512,256]{1,0:T(8,128)}, f32[512,256]{1,0:T(8,128)}, u32[]{:S(2)}, u32[]{:S(2)}) collective-permute-start(f32[512,256]{1,0:T(8,128)} %get-tuple-element.24), channel_id=1, source_target_pairs={{8,16},{16,8},{9,17},{17,9},{10,18},{18,10},{11,19},{19,11},{12,20... | collective-permute-start | bytes 1572872 | tf_op jit(solution)/shard_map/ppermute | solution.py:191
  96.5 23.8 %collective-permute-start.19 = (f32[512,256]{1,0:T(8,128)}, f32[512,256]{1,0:T(8,128)}, u32[]{:S(2)}, u32[]{:S(2)}) collective-permute-start(f32[512,256]{1,0:T(8,128)} %get-tuple-element.20), channel_id=1, source_target_pairs={{8,16},{16,8},{9,17},{17,9},{10,18},{18,10},{11,19},{19,11},{12,20... | collective-permute-start | bytes 1572872 | tf_op jit(solution)/shard_map/ppermute | solution.py:191
  103.9 16.3 %collective-permute-start.18 = (f32[512,256]{1,0:T(8,128)}, f32[512,256]{1,0:T(8,128)}, u32[]{:S(2)}, u32[]{:S(2)}) collective-permute-start(f32[512,256]{1,0:T(8,128)} %collective-permute-done.17), channel_id=1, source_target_pairs={{8,16},{16,8},{9,17},{17,9},{10,18},{18,10},{11,19},{19,11},{12,20... | collective-permute-start | bytes 1572872 | tf_op jit(solution)/shard_map/ppermute | solution.py:192
  108.1 24.6 %collective-permute-start.32 = (f32[512,256]{1,0:T(8,128)}, f32[512,256]{1,0:T(8,128)}, u32[]{:S(2)}, u32[]{:S(2)}) collective-permute-start(f32[512,256]{1,0:T(8,128)} %select_select_fusion.1), channel_id=1, source_target_pairs={{8,0},{16,24},{9,1},{17,25},{10,2},{18,26},{11,3},{19,27},{12,4},{... | collective-permute-start | bytes 1572872 | tf_op jit(solution)/shard_map/ppermute | solution.py:194
  109.6 42.9 %collective-permute-start.27 = (f32[512,256]{1,0:T(8,128)}, f32[512,256]{1,0:T(8,128)S(1)}, u32[]{:S(2)}, u32[]{:S(2)}) collective-permute-start(f32[512,256]{1,0:T(8,128)} %copy-done.7), channel_id=1, source_target_pairs={{8,16},{16,8},{9,17},{17,9},{10,18},{18,10},{11,19},{19,11},{12,20... | collective-permute-start | bytes 1572872 | tf_op jit(solution)/shard_map/ppermute | solution.py:191
  110.3 40.2 %collective-permute-start.25 = (f32[512,256]{1,0:T(8,128)}, f32[512,256]{1,0:T(8,128)}, u32[]{:S(2)}, u32[]{:S(2)}) collective-permute-start(f32[512,256]{1,0:T(8,128)} %copy-done.7), channel_id=1, source_target_pairs={{0,8},{24,16},{1,9},{25,17},{2,10},{26,18},{3,11},{27,19},{4,12},{... | collective-permute-start | bytes 1572872 | tf_op jit(solution)/shard_map/ppermute | solution.py:190
  121.4 29.7 %collective-permute-start.20 = (f32[512,256]{1,0:T(8,128)S(1)}, f32[512,256]{1,0:T(8,128)S(1)}, u32[]{:S(2)}, u32[]{:S(2)}) collective-permute-start(f32[512,256]{1,0:T(8,128)S(1)} %select_select_fusion.4), channel_id=1, source_target_pairs={{8,0},{16,24},{9,1},{17,25},{10,2},{18,26},{11,3},{19,27},{12,4},{... | collective-permute-start | bytes 1572872 | tf_op jit(solution)/shard_map/ppermute | solution.py:194
  134.1 20.0 %collective-permute-start.34 = (f32[512,256]{1,0:T(8,128)S(1)}, f32[512,256]{1,0:T(8,128)S(1)}, u32[]{:S(2)}, u32[]{:S(2)}) collective-permute-start(f32[512,256]{1,0:T(8,128)S(1)} %select_add_fusion.1), channel_id=1, source_target_pairs={{0,4},{1,5},{2,6},{3,7},{4,0},{5,1},{6,2},{7,3},{8,12},{9,13},{10,... | collective-permute-start | bytes 1572872 | tf_op jit(solution)/shard_map/ppermute | solution.py:160
  134.2 22.9 %collective-permute-start.13 = (f32[512,256]{1,0:T(8,128)}, f32[512,256]{1,0:T(8,128)}, u32[]{:S(2)}, u32[]{:S(2)}) collective-permute-start(f32[512,256]{1,0:T(8,128)} %get-tuple-element.18), channel_id=1, source_target_pairs={{0,8},{24,16},{1,9},{25,17},{2,10},{26,18},{3,11},{27,19},{4,12},{... | collective-permute-start | bytes 1572872 | tf_op jit(solution)/shard_map/ppermute | solution.py:190
  152.5 19.2 %collective-permute-start.21 = (f32[512,256]{1,0:T(8,128)S(1)}, f32[512,256]{1,0:T(8,128)}, u32[]{:S(2)}, u32[]{:S(2)}) collective-permute-start(f32[512,256]{1,0:T(8,128)S(1)} %select_add_fusion.3), channel_id=1, source_target_pairs={{0,2},{1,3},{2,0},{3,1},{4,6},{5,7},{6,4},{7,5},{8,10},{9,11},{10,... | collective-permute-start | bytes 1572872 | tf_op jit(solution)/shard_map/ppermute | solution.py:160
  154.1 28.8 %collective-permute-start.35 = (f32[512,256]{1,0:T(8,128)S(1)}, f32[512,256]{1,0:T(8,128)}, u32[]{:S(2)}, u32[]{:S(2)}) collective-permute-start(f32[512,256]{1,0:T(8,128)S(1)} %collective-permute-done.34), channel_id=1, source_target_pairs={{0,2},{1,3},{2,0},{3,1},{4,6},{5,7},{6,4},{7,5},{8,10},{9,11},{10,... | collective-permute-start | bytes 1572872 | tf_op jit(solution)/shard_map/ppermute | solution.py:160
  157.1 29.9 %collective-permute-start.15 = (f32[512,256]{1,0:T(8,128)}, f32[512,256]{1,0:T(8,128)S(1)}, u32[]{:S(2)}, u32[]{:S(2)}) collective-permute-start(f32[512,256]{1,0:T(8,128)} %get-tuple-element.18), channel_id=1, source_target_pairs={{8,16},{16,8},{9,17},{17,9},{10,18},{18,10},{11,19},{19,11},{12,20... | collective-permute-start | bytes 1572872 | tf_op jit(solution)/shard_map/ppermute | solution.py:191
  157.8 34.0 %collective-permute-start.14 = (f32[512,256]{1,0:T(8,128)}, f32[512,256]{1,0:T(8,128)S(1)}, u32[]{:S(2)}, u32[]{:S(2)}) collective-permute-start(f32[512,256]{1,0:T(8,128)} %collective-permute-done.13), channel_id=1, source_target_pairs={{8,16},{16,8},{9,17},{17,9},{10,18},{18,10},{11,19},{19,11},{12,20... | collective-permute-start | bytes 1572872 | tf_op jit(solution)/shard_map/ppermute | solution.py:192
  160.6 43.2 %collective-permute-start.28 = (f32[512,256]{1,0:T(8,128)}, f32[512,256]{1,0:T(8,128)}, u32[]{:S(2)}, u32[]{:S(2)}) collective-permute-start(f32[512,256]{1,0:T(8,128)} %select_select_fusion.2), channel_id=1, source_target_pairs={{8,0},{16,24},{9,1},{17,25},{10,2},{18,26},{11,3},{19,27},{12,4},{... | collective-permute-start | bytes 1572872 | tf_op jit(solution)/shard_map/ppermute | solution.py:194
  171.7 22.6 %collective-permute-start.22 = (f32[512,256]{1,0:T(8,128)S(1)}, f32[512,256]{1,0:T(8,128)S(1)}, u32[]{:S(2)}, u32[]{:S(2)}) collective-permute-start(f32[512,256]{1,0:T(8,128)S(1)} %select_add_fusion.3), channel_id=1, source_target_pairs={{0,4},{1,5},{2,6},{3,7},{4,0},{5,1},{6,2},{7,3},{8,12},{9,13},{10,... | collective-permute-start | bytes 1572872 | tf_op jit(solution)/shard_map/ppermute | solution.py:160
  182.9 14.9 %collective-permute-start.23 = (f32[512,256]{1,0:T(8,128)}, f32[512,256]{1,0:T(8,128)S(1)}, u32[]{:S(2)}, u32[]{:S(2)}) collective-permute-start(f32[512,256]{1,0:T(8,128)} %collective-permute-done.21), channel_id=1, source_target_pairs={{0,4},{1,5},{2,6},{3,7},{4,0},{5,1},{6,2},{7,3},{8,12},{9,13},{10,... | collective-permute-start | bytes 1572872 | tf_op jit(solution)/shard_map/ppermute | solution.py:160
  187.1 16.7 %collective-permute-start.36 = (f32[512,256]{1,0:T(8,128)}, f32[512,256]{1,0:T(8,128)}, u32[]{:S(2)}, u32[]{:S(2)}) collective-permute-start(f32[512,256]{1,0:T(8,128)} %select_select_fusion), channel_id=1, source_target_pairs={{0,1},{1,0},{2,3},{3,2},{4,5},{5,4},{6,7},{7,6},{8,9},{9,8},{10,11... | collective-permute-start | bytes 1572872 | tf_op jit(solution)/shard_map/ppermute | solution.py:160
  192.8 15.8 %collective-permute-start.16 = (f32[512,256]{1,0:T(8,128)}, f32[512,256]{1,0:T(8,128)}, u32[]{:S(2)}, u32[]{:S(2)}) collective-permute-start(f32[512,256]{1,0:T(8,128)} %select_select_fusion.5), channel_id=1, source_target_pairs={{8,0},{16,24},{9,1},{17,25},{10,2},{18,26},{11,3},{19,27},{12,4},{... | collective-permute-start | bytes 1572872 | tf_op jit(solution)/shard_map/ppermute | solution.py:194
  (34 other events, 307.6 us)

commit v2 on v0

v2 whole, which is shorter than its diff:
```python
import functools

import jax
import jax.numpy as jnp
from jax import lax
from jax.experimental import pallas as pl
from jax.experimental.pallas import tpu as pltpu
from jax.sharding import PartitionSpec as P

F32 = jnp.float32
BF16 = jnp.bfloat16
VMEM_BYTES = 48 * 1024 * 1024


def split(value):
    high = value.astype(BF16)
    low = (value - high.astype(F32)).astype(BF16)
    return high, low


def dot(left, right):
    return jnp.dot(left, right, preferred_element_type=F32)


def product(left_both, right_high, right_low):
    half = left_both.shape[0] // 2
    over_high = dot(left_both, right_high)
    over_low = dot(left_both[:half], right_low)
    return over_high[:half] + (over_high[half:] + over_low)


def slot_at(coords, place, block_cols, slot_count):
    found = jnp.int32(-1)
    for slot in range(slot_count):
        hit = coords[slot, 0] * block_cols + coords[slot, 1] == place
        found = jnp.where(hit, jnp.int32(slot), found)
    return found


def left_kernel(block_of, block_cols, slot_count, *refs):
    me, coords, counts, tile_ref, q_ref = refs[:5]
    out, q_both = refs[-2:]
    group, column = pl.program_id(0), pl.program_id(1)
    width = q_both.shape[0] // 2

    @pl.when(column == 0)
    def _():
        high, low = split(q_ref[...].T)
        q_both[:width] = high
        q_both[width:] = low

    place = block_of(me, group) * block_cols + column
    slot = slot_at(coords, place, block_cols, slot_count)
    live = (slot >= 0) & (slot < counts[0])

    @pl.when(live)
    def _():
        high, low = split(tile_ref[0])
        total_high, total_low = split(product(q_both[...], high, low))
        out[0, :width] = total_high
        out[0, width:] = total_low

    @pl.when(jnp.logical_not(live))
    def _():
        out[...] = jnp.zeros_like(out)


def left_products(me, coords, counts, tiles, q_rows, block_of, block_rows, block_cols, before):
    slot_count, tile_order, _ = tiles.shape
    width = q_rows.shape[1]
    groups = q_rows.shape[0] // tile_order
    positions = block_rows * block_cols

    def tile_at(g, b, me_ref, coords_ref, counts_ref):
        place = block_of(me_ref, g) * block_cols + b
        return jnp.maximum(slot_at(coords_ref, place, block_cols, slot_count), 0), 0, 0

    def out_at(g, b, me_ref, coords_ref, counts_ref):
        return block_of(me_ref, g) * block_cols + b, 0, 0

    in_specs = [
        pl.BlockSpec((1, tile_order, tile_order), tile_at),
        pl.BlockSpec((tile_order, width), lambda g, b, *_: (g, 0)),
    ]
    operands = [me, coords, counts, tiles, q_rows]
    aliases = {}
    if before is not None:
        in_specs.append(pl.BlockSpec(memory_space=pl.ANY))
        aliases = {len(operands): 0}
        operands.append(before)
    return pl.pallas_call(
        functools.partial(left_kernel, block_of, block_cols, slot_count),
        grid_spec=pltpu.PrefetchScalarGridSpec(
            num_scalar_prefetch=3,
            grid=(groups, block_cols),
            in_specs=in_specs,
            out_specs=pl.BlockSpec((1, 2 * width, tile_order), out_at),
            scratch_shapes=[pltpu.VMEM((2 * width, tile_order), BF16)],
        ),
        out_shape=jax.ShapeDtypeStruct((positions, 2 * width, tile_order), BF16),
        input_output_aliases=aliases,
        compiler_params=pltpu.CompilerParams(vmem_limit_bytes=VMEM_BYTES),
        cost_estimate=pl.CostEstimate(
            flops=12 * groups * block_cols * width * tile_order * tile_order,
            bytes_accessed=4 * groups * block_cols * tile_order * (tile_order + width),
            transcendentals=0,
        ),
        name="left_products",
    )(*operands)


def mates(me, row_partner, col_partner):
    row, col = me[0], me[1]
    row_mate = row_partner[col, row]
    return row, col, row_mate, col_partner[row, col], col_partner[row_mate, col]


def place_of(given, block_rows, block_cols, me, row_partner, col_partner, step):
    row, col, row_mate, col_mate, row_mates_col = mates(me, row_partner, col_partner)
    half_rows, half_cols = block_rows // 2, block_cols // 2
    quarter, inside = step // (half_rows * half_cols), step % (half_rows * half_cols)
    if given:
        row_half, keeps = row_mate > row, col > row_mates_col
    else:
        row_half, keeps = row > row_mate, col > col_mate
    col_half = jnp.where(keeps, quarter, 1 - quarter)
    block_row = jnp.where(row_half, half_rows, 0) + inside // half_cols
    block_col = col_half * half_cols + inside % half_cols
    return block_row, block_col


def right_kernel(given, block_rows, block_cols, shard_places, groups, *refs):
    me, row_partner, col_partner, w_ref = refs[:4]
    pieces = refs[4 : 4 + sum(groups)]
    out, p_high, p_low = refs[4 + sum(groups) :]
    step = pl.program_id(0)
    tile_order = w_ref.shape[2]
    depth = pieces[0].shape[0]

    @pl.when(step == 0)
    def _():
        at = 0
        for place, count in zip(shard_places(me), groups):
            value = pieces[at][...]
            for other in range(1, count):
                value = value + pieces[at + other][...]
            at += count
            rows = pl.ds(pl.multiple_of(place * depth, depth), depth)
            p_high[rows, :], p_low[rows, :] = split(value)

    _, block_col = place_of(given, block_rows, block_cols, me, row_partner, col_partner, step)
    rows = pl.ds(pl.multiple_of(block_col * tile_order, tile_order), tile_order)
    out[0] = product(w_ref[0], p_high[rows, :], p_low[rows, :])


def right_products(given, tables, w, shards, shard_places, block_rows, block_cols):
    _, both, tile_order = w.shape
    width = both // 2
    depth = shards[0][0].shape[0]
    half_rows, half_cols = block_rows // 2, block_cols // 2
    per_quarter = half_rows * half_cols
    steps = 2 * per_quarter
    groups = [len(shard) for shard in shards]
    place = functools.partial(place_of, given, block_rows, block_cols)

    def w_at(i, *refs):
        block_row, block_col = place(*refs, i)
        return block_row * block_cols + block_col, 0, 0

    def out_at(i, *refs):
        inside = i % per_quarter
        return i // per_quarter, inside // half_cols, inside % half_cols

    whole = pl.BlockSpec((depth, width), lambda i, *_: (0, 0))
    return pl.pallas_call(
        functools.partial(
            right_kernel, given, block_rows, block_cols, shard_places, groups
        ),
        grid_spec=pltpu.PrefetchScalarGridSpec(
            num_scalar_prefetch=3,
            grid=(steps,),
            in_specs=[pl.BlockSpec((1, both, tile_order), w_at)] + [whole] * sum(groups),
            out_specs=pl.BlockSpec((1, width, width), out_at),
            scratch_shapes=[pltpu.VMEM((len(shards) * depth, width), BF16)] * 2,
        ),
        out_shape=jax.ShapeDtypeStruct((2, half_rows * width, half_cols * width), F32),
        compiler_params=pltpu.CompilerParams(vmem_limit_bytes=VMEM_BYTES),
        cost_estimate=pl.CostEstimate(
            flops=12 * steps * width * width * tile_order,
            bytes_accessed=4 * steps * width * (tile_order + width),
            transcendentals=0,
        ),
        name="right_products",
    )(*tables, w, *[piece for shard in shards for piece in shard])


def flip(value, axis, size, mask):
    return lax.ppermute(value, axis, [(i, i ^ mask) for i in range(size)])


def gather_prolong(shard, axis, size):
    if size != 4:
        gathered = lax.all_gather(shard, axis)
        return [[gathered[i]] for i in range(size)], lambda me: list(range(size))
    mate = flip(shard, axis, size, 1)
    over = lax.ppermute(shard, axis, [(1, 2), (2, 1)])
    mate_over = lax.ppermute(mate, axis, [(1, 2), (2, 1)])
    handed = lax.ppermute(over, axis, [(1, 0), (2, 3)])
    mate_handed = lax.ppermute(mate_over, axis, [(1, 0), (2, 3)])

    def places(me):
        row = me[0]
        return [row, row ^ 1, jnp.where(row < 2, 2, 1), jnp.where(row < 2, 3, 0)]

    return [[shard], [mate], [over, handed], [mate_over, mate_handed]], places


def pair_switch(mine, mate, size, branch, *operands):
    if size == 2:
        return branch(1, *operands)
    branches = [functools.partial(branch, mask) for mask in range(1, size)]
    return lax.switch((mine ^ mate) - 1, branches, *operands)


def solution(mesh):
    n_row = mesh.shape["row"]
    n_col = mesh.shape["col"]

    def body(tiles, coords, counts, restrict, prolong, row_partner, col_partner):
        tile_order = tiles.shape[1]
        q_depth = restrict.shape[0]
        block_rows = q_depth * n_col // tile_order
        block_cols = prolong.shape[0] * n_row // tile_order
        row = lax.axis_index("row").astype(jnp.int32)
        col = lax.axis_index("col").astype(jnp.int32)
        me = jnp.stack([row, col])

        shards, shard_places = gather_prolong(prolong, "row", n_row)

        left = functools.partial(left_products, me, coords, counts, tiles)
        if n_col == 8 and tile_order == 2 * q_depth:
            mate = flip(restrict, "col", n_col, 1)
            odd = (col & 1) == 1
            own = jnp.concatenate(
                [jnp.where(odd, mate, restrict), jnp.where(odd, restrict, mate)], axis=0
            )
            w = None
            for chip in range(n_col // 2):
                block = own if chip == 0 else flip(own, "col", n_col, 2 * chip)
                w = left(block, lambda ref, g, chip=chip: (ref[1] // 2) ^ chip, block_rows, block_cols, w)
        else:
            blocks = lax.all_gather(restrict, "col", axis=0, tiled=True)
            w = left(blocks, lambda ref, g: g, block_rows, block_cols, None)

        tables = (me, row_partner, col_partner)
        given = right_products(True, tables, w, shards, shard_places, block_rows, block_cols)

        def row_branch(mask, given, w, shards):
            received = flip(given, "row", n_row, mask)
            kept = right_products(False, tables, w, shards, shard_places, block_rows, block_cols)
            return received, kept

        def col_branch(mask, section):
            return flip(section, "col", n_col, mask)

        received, kept = pair_switch(row, row_partner[col, row], n_row, row_branch, given, w, shards)
        section = kept[0] + received[0]
        section = pair_switch(col, col_partner[row, col], n_col, col_branch, section)
        return (kept[1] + received[1]) + section

    in_specs = (
        P(("row", "col"), None, None),
        P(("row", "col"), None),
        P(("row", "col")),
        P(("row", "col"), None),
        P(("col", "row"), None),
        P(),
        P(),
    )
    return jax.shard_map(
        body, mesh=mesh, in_specs=in_specs, out_specs=P("row", "col"), check_vma=False
    )
```

time: 457 us -> 179 us (0.39)
  waiting for transfers between devices: 275 us -> 118 us
  matrix products: 83.4 us -> 0 us
  loops' own time: 52.4 us -> 0.05 us
  Pallas kernels: 0 us -> 31.8 us
  starting transfers between devices: 0.12 us -> 13.9 us
  between operations: 15.9 us -> 2.17 us
  local copies, waits for them, and re-layouts: 16 us -> 3.9 us
  other arithmetic: 11.4 us -> 5.7 us
    all_gather x4 -> x0, waiting for transfers between devices: 274 us -> none  [the longest x1 147 us: body(): gathered = lax.all_gather(given, 'row', axis=0, tiled=True)]
    ppermute x0 -> x11, waiting for transfers between devices: none -> 118 us  [the longest x7 114 us: flip(): return lax.ppermute(value, axis, [(i, i ^ mask) for i in range(size)])]
    dot_general x32 -> x0, matrix products: 83.4 us -> none  [the longest x16 45.8 us: add_slot(): product = jnp.dot(left.T, applied, precision=lax.Precision.HIGHEST)]
    another operation x1 -> x2, loops' own time: 52.4 us -> 0.05 us  [pair_switch(): return lax.switch((mine ^ mate) - 1, branches, *operands)]
    pallas_call x0 -> x6, Pallas kernels: none -> 31.8 us  [the longest x4 18 us: left_products(): pl.pallas_call(functools.partial(left_kernel, block_of, block_cols, slot_...]
    ppermute x0 -> x11, starting transfers between devices: none -> 13.9 us  [the longest x7 9.96 us: flip(): return lax.ppermute(value, axis, [(i, i ^ mask) for i in range(size)])]
    dynamic_slice x18 -> x2, local copies, waits for them, and re-layouts: 13.5 us -> 1.3 us  [the longest x1 0.65 us: body(): col_partner[row, col]]
  transfers between devices with their start and end apart: 4 -> 11, of which waited for: 4 -> 5; matrix products, arithmetic and copies ran while one was open for 1% -> 2% of each run, Pallas kernels for 0% -> 15%
where the time goes in v2:
time: 179 us; the launch traced here: 176 us
  waiting for transfers between devices  118 us (66%)
  Pallas kernels  31.8 us (18%)
  starting transfers between devices  13.9 us (8%)
  other arithmetic  5.7 us (3%)
  local copies, waits for them, and re-layouts  3.9 us (2%)
  between operations  2.17 us (1%)
    ppermute x7, waiting for transfers between devices, flip(): return lax.ppermute(value, axis, [(i, i ^ mask) for i in range(size)])  114 us
    pallas_call x4, Pallas kernels, left_products(): pl.pallas_call(functools.partial(left_kernel, block_of, block_cols, slot_...  18 us
    pallas_call x2, Pallas kernels, right_products(): pl.pallas_call(functools.partial(right_kernel, given, block_rows, block_c...  13.8 us
    ppermute x7, starting transfers between devices, flip(): return lax.ppermute(value, axis, [(i, i ^ mask) for i in range(size)])  9.96 us
    ppermute x1, waiting for transfers between devices, gather_prolong(): mate_handed = lax.ppermute(mate_over, axis, [(1, 0), (2, 3)])  4.64 us
  transfers between devices with their start and end apart: 11, of which 5 were waited for; matrix products, arithmetic and copies ran while one was open for 2% of the time, Pallas kernels for 15%

profile of v2, /device:TPU:3, one launch (start us, length us, event | category | flops | bytes accessed | tf_op | source)
XLA Modules:
  0.0 175.7 jit_solution(2178306396276467802)
XLA Ops:
  0.0 0.7 collective-permute-start.10
  0.8 0.7 collective-permute-start.15
  1.4 3.9 %collective-permute-start.14 = (f32[512,256]{1,0:T(8,128)}, f32[512,256]{1,0:T(8,128)S(1)}, u32[]{:S(2)}, u32[]{:S(2)}) collective-permute-start(f32[512,256]{1,0:T(8,128)} %refs_4_.1), channel_id=1, source_target_pairs={{0,8},{8,0},{16,24},{24,16},{1,9},{9,1},{17,25},{25,17},{2,10},{10... | collective-permute-start | bytes 1572872 | tf_op jit(solution)/shard_map/ppermute | solution.py:198
  5.3 1.0 broadcast_select_fusion.1
  6.4 0.3 collective-permute-start.13
  7.4 0.6 dynamic_slice.6
  8.1 0.6 dynamic_slice.7
  10.1 0.1 copy.14.refs_1_
  10.2 1.2 collective-permute-start.12
  11.5 1.2 collective-permute-start.11
  12.6 5.0 %collective-permute-done.14.refs_5_ = f32[512,256]{1,0:T(8,128)S(1)} collective-permute-done((f32[512,256]{1,0:T(8,128)}, f32[512,256]{1,0:T(8,128)S(1)}, u32[]{:S(2)}, u32[]{:S(2)}) %collective-permute-start.14) | collective-permute-done | bytes 524320 | tf_op jit(solution)/shard_map/ppermute | solution.py:198
  17.6 0.7 collective-permute-start.17
  18.3 4.4 %left_products.4.refs_5_ = bf16[16,512,512]{2,1,0:T(8,128)(2,1)S(1)} custom-call(s32[2]{0:T(128)S(1)} %pad_add_fusion.refs_0_, s32[16,2]{1,0:T(8,128)S(1)} %copy.14.refs_1_, s32[1]{0:T(128)S(6)} %copy.35.refs_2_, f32[16,512,512]{2,1,0:T(8,128)} %refs_3_.7, f32[512,256]{1,0:T(8,128)S(1)} %pad_maximum_fusion.refs_4_), custom_call_target="tpu_custom_call" | custom-call | flops 3221225472 | bytes 6291456 | tf_op jit(solution)/shard_map/left_products/pallas_call | solution.py:91
  22.7 1.3 collective-permute-start.16
  24.0 4.6 %left_products.5.refs_5_ = bf16[16,512,512]{2,1,0:T(8,128)(2,1)S(1)} custom-call(s32[2]{0:T(128)S(1)} %pad_add_fusion.refs_0_, s32[16,2]{1,0:T(8,128)S(1)} %copy.14.refs_1_, s32[1]{0:T(128)S(6)} %copy.35.refs_2_, f32[16,512,512]{2,1,0:T(8,128)} %refs_3_.7, f32[512,256]{1,0:T(8,128)S(1)} %collective-permute-done.13.refs_4_, ...), custom_call_target="tpu_custom_call", output_to_operand_aliasing={{}: (5, {})} | custom-call | flops 3221225472 | bytes 6291456 | tf_op jit(solution)/shard_map/left_products/pallas_call | solution.py:91
  28.6 1.3 collective-permute-start.18
  29.9 4.2 %collective-permute-done.12.refs_4_ = f32[512,256]{1,0:T(8,128)S(1)} collective-permute-done((f32[512,256]{1,0:T(8,128)S(1)}, f32[512,256]{1,0:T(8,128)S(1)}, u32[]{:S(2)}, u32[]{:S(2)}) %collective-permute-start.12) | collective-permute-done | bytes 524320 | tf_op jit(solution)/shard_map/ppermute | solution.py:198
  34.1 4.6 %left_products.6.refs_5_ = bf16[16,512,512]{2,1,0:T(8,128)(2,1)S(1)} custom-call(s32[2]{0:T(128)S(1)} %pad_add_fusion.refs_0_, s32[16,2]{1,0:T(8,128)S(1)} %copy.14.refs_1_, s32[1]{0:T(128)S(6)} %copy.35.refs_2_, f32[16,512,512]{2,1,0:T(8,128)} %refs_3_.7, f32[512,256]{1,0:T(8,128)S(1)} %collective-permute-done.12.refs_4_, ...), custom_call_target="tpu_custom_call", output_to_operand_aliasing={{}: (5, {})} | custom-call | flops 3221225472 | bytes 6291456 | tf_op jit(solution)/shard_map/left_products/pallas_call | solution.py:91
  38.7 4.5 %left_products.7.refs_3_ = bf16[16,512,512]{2,1,0:T(8,128)(2,1)S(1)} custom-call(s32[2]{0:T(128)S(1)} %pad_add_fusion.refs_0_, s32[16,2]{1,0:T(8,128)S(1)} %copy.14.refs_1_, s32[1]{0:T(128)S(6)} %copy.35.refs_2_, f32[16,512,512]{2,1,0:T(8,128)} %refs_3_.7, f32[512,256]{1,0:T(8,128)S(1)} %collective-permute-done.11.refs_4_, ...), custom_call_target="tpu_custom_call", output_to_operand_aliasing={{}: (5, {})} | custom-call | flops 3221225472 | bytes 6291456 | tf_op jit(solution)/shard_map/left_products/pallas_call | solution.py:91
  43.2 4.6 %collective-permute-done.18.refs_9_ = f32[512,256]{1,0:T(8,128)S(1)} collective-permute-done((f32[512,256]{1,0:T(8,128)S(1)}, f32[512,256]{1,0:T(8,128)S(1)}, u32[]{:S(2)}, u32[]{:S(2)}) %collective-permute-start.18) | collective-permute-done | bytes 524320 | tf_op jit(solution)/shard_map/ppermute | solution.py:209
  47.8 6.0 %right_products.7 = f32[2,512,512]{2,1,0:T(8,128)} custom-call(s32[2]{0:T(128)S(1)} %pad_add_fusion.refs_0_, s32[8,4]{1,0:T(8,128)S(1)} %copy.15.refs_1_, s32[4,8]{1,0:T(4,128)S(1)} %copy-done.9, bf16[16,512,512]{2,1,0:T(8,128)(2,1)S(1)} %left_products.7.refs_3_, f32[512,256]{1,0:T(8,128)S(1)} %copy-done.3, f32[512,256]{1,0:T(8,128)S(1)} %collective-permute-done.14.refs_5_, ...), custom_call_target="tpu_custom_call" | custom-call | flops 3221225472 | bytes 6291456 | tf_op jit(solution)/shard_map/right_products/pallas_call | solution.py:175
  53.8 91.9 %conditional.2 = (f32[2,512,512]{2,1,0:T(8,128)}, f32[2,512,512]{2,1,0:T(8,128)S(1)}) conditional(s32[]{:T(128)} %clamp.6, (f32[2,512,512]{2,1,0:T(8,128)}, s32[2]{0:T(128)S(1)}, s32[8,4]{0,1:T(4,128)S(1)}, s32[4,8]{1,0:T(4,128)S(1)}, bf16[16,512,512]{2,1,0:T(8,128)(2,1)S(1)}, /*index=5*/f32[512,256]{1,0:T(8,128)S(1)}, ...), branch_computations={%region_0.1_spmd, %region_1.2_spmd, %region_2.3_spmd} | conditional | flops 3221225472 | bytes 50332016 | solution.py:222
  53.8 2.6 %collective-permute-start.1 = (f32[2,512,512]{2,1,0:T(8,128)}, f32[2,512,512]{2,1,0:T(8,128)}, u32[]{:S(2)}, u32[]{:S(2)}) collective-permute-start(f32[2,512,512]{2,1,0:T(8,128)} %get-tuple-element.97), channel_id=1, source_target_pairs={{0,16},{8,24},{16,0},{24,8},{1,17},{9,25},{17,1},{25,9},{2,18},{10... | collective-permute-start | bytes 6291464 | tf_op jit(solution)/shard_map/cond/branch_1_fun/ppermute | solution.py:198
  56.3 0.7 copy-done.1
  57.1 0.3 copy-done.5
  57.4 7.8 %right_products.5 = f32[2,512,512]{2,1,0:T(8,128)S(1)} custom-call(s32[2]{0:T(128)S(1)} %get-tuple-element.98.refs_0_, s32[8,4]{1,0:T(8,128)S(1)} %copy.17.refs_1_, s32[4,8]{1,0:T(4,128)S(1)} %get-tuple-element.100.refs_2_, bf16[16,512,512]{2,1,0:T(8,128)(2,1)} %copy-done.1, f32[512,256]{1,0:T(8,128)S(1)} %get-tuple-element.102.refs_4_, ...), custom_call_target="tpu_custom_call" | custom-call | flops 3221225472 | bytes 6291456 | tf_op jit(solution)/shard_map/cond/branch_1_fun/right_products/pallas_call | solution.py:175
  65.2 80.5 %collective-permute-done.1 = f32[2,512,512]{2,1,0:T(8,128)} collective-permute-done((f32[2,512,512]{2,1,0:T(8,128)}, f32[2,512,512]{2,1,0:T(8,128)}, u32[]{:S(2)}, u32[]{:S(2)}) %collective-permute-start.1) | collective-permute-done | bytes 2097184 | tf_op jit(solution)/shard_map/cond/branch_1_fun/ppermute | solution.py:198
  145.7 1.3 copy-done.7
  147.1 1.4 add_bitcast_fusion
  148.5 24.1 %conditional.3 = (f32[512,512]{1,0:T(8,128)}) conditional(s32[]{:T(128)} %clamp.7, f32[512,512]{1,0:T(8,128)S(1)} %add_bitcast_fusion, f32[512,512]{1,0:T(8,128)S(1)} %add_bitcast_fusion, f32[512,512]{1,0:T(8,128)S(1)} %add_bitcast_fusion, f32[512,512]{1,0:T(8,128)S(1)} %add_bitcast_fusion, ...), branch_computations={%region_3.4_spmd, %region_4.5_spmd, %region_5.6_spmd, %region_6.7_... | conditional | bytes 4194352 | solution.py:222
  148.6 23.9 %collective-permute-done.9 = f32[512,512]{1,0:T(8,128)} collective-permute-done((f32[512,512]{1,0:T(8,128)S(1)}, f32[512,512]{1,0:T(8,128)}, u32[]{:S(2)}, u32[]{:S(2)}) %collective-permute-start.9) | collective-permute-done | bytes 1048608 | tf_op jit(solution)/shard_map/cond/branch_6_fun/ppermute | solution.py:198
  172.5 3.2 %bitcast_add_fusion = f32[512,512]{1,0:T(8,128)} fusion(f32[512,512]{1,0:T(8,128)} %get-tuple-element.164, f32[2,512,512]{2,1,0:T(8,128)} %get-tuple-element.122, f32[2,512,512]{2,1,0:T(8,128)} %copy-done.7), kind=kLoop, calls=%fused_computation | loop fusion | flops 524288 | bytes 4194304 | tf_op jit(solution)/shard_map/add | solution.py:269
  (22 shorter events, 0.4 us)
Async XLA Ops:
  0.0 7.3 %copy-start.8 = (s32[8,4]{0,1:T(4,128)S(1)}, s32[8,4]{0,1:T(4,128)}, u32[]{:S(2)}) copy-start(s32[8,4]{0,1:T(4,128)} %param.22) | copy-start | bytes 388
  0.0 8.1 %copy-start.9 = (s32[4,8]{1,0:T(4,128)S(1)}, s32[4,8]{1,0:T(4,128)}, u32[]{:S(2)}) copy-start(s32[4,8]{1,0:T(4,128)} %refs_2_.5) | copy-start | bytes 388
  0.0 10.1 %copy-start.10 = (s32[16,2]{0,1:T(2,128)S(1)}, s32[16,2]{0,1:T(2,128)}, u32[]{:S(2)}) copy-start(s32[16,2]{0,1:T(2,128)} %param.18) | copy-start | bytes 388
  0.0 5.3 %collective-permute-start.10 = (f32[256,256]{1,0:T(8,128)}, f32[256,256]{1,0:T(8,128)S(1)}, u32[]{:S(2)}, u32[]{:S(2)}) collective-permute-start(f32[256,256]{1,0:T(8,128)} %param.20), channel_id=1, source_target_pairs={{0,1},{1,0},{2,3},{3,2},{4,5},{5,4},{6,7},{7,6},{8,9},{9,8},{10,11... | collective-permute-start | bytes 786440 | tf_op jit(solution)/shard_map/ppermute | solution.py:198
  0.8 21.9 %collective-permute-start.15 = (f32[512,256]{1,0:T(8,128)}, f32[512,256]{1,0:T(8,128)S(1)}, u32[]{:S(2)}, u32[]{:S(2)}) collective-permute-start(f32[512,256]{1,0:T(8,128)} %refs_4_.1), channel_id=1, source_target_pairs={{8,16},{16,8},{9,17},{17,9},{10,18},{18,10},{11,19},{19,11},{12,20... | collective-permute-start | bytes 1572872 | tf_op jit(solution)/shard_map/ppermute | solution.py:206
  1.4 16.2 %collective-permute-start.14 = (f32[512,256]{1,0:T(8,128)}, f32[512,256]{1,0:T(8,128)S(1)}, u32[]{:S(2)}, u32[]{:S(2)}) collective-permute-start(f32[512,256]{1,0:T(8,128)} %refs_4_.1), channel_id=1, source_target_pairs={{0,8},{8,0},{16,24},{24,16},{1,9},{9,1},{17,25},{25,17},{2,10},{10... | collective-permute-start | bytes 1572872 | tf_op jit(solution)/shard_map/ppermute | solution.py:198
  6.4 17.6 %collective-permute-start.13 = (f32[512,256]{1,0:T(8,128)S(1)}, f32[512,256]{1,0:T(8,128)S(1)}, u32[]{:S(2)}, u32[]{:S(2)}) collective-permute-start(f32[512,256]{1,0:T(8,128)S(1)} %pad_maximum_fusion.refs_4_), channel_id=1, source_target_pairs={{0,2},{1,3},{2,0},{3,1},{4,6},{5,7},{6,4},{7,5},{8,10},{9,11},{10,... | collective-permute-start | bytes 1572872 | tf_op jit(solution)/shard_map/ppermute | solution.py:198
  10.2 23.8 %collective-permute-start.12 = (f32[512,256]{1,0:T(8,128)S(1)}, f32[512,256]{1,0:T(8,128)S(1)}, u32[]{:S(2)}, u32[]{:S(2)}) collective-permute-start(f32[512,256]{1,0:T(8,128)S(1)} %pad_maximum_fusion.refs_4_), channel_id=1, source_target_pairs={{0,4},{1,5},{2,6},{3,7},{4,0},{5,1},{6,2},{7,3},{8,12},{9,13},{10,... | collective-permute-start | bytes 1572872 | tf_op jit(solution)/shard_map/ppermute | solution.py:198
  11.5 27.2 %collective-permute-start.11 = (f32[512,256]{1,0:T(8,128)S(1)}, f32[512,256]{1,0:T(8,128)S(1)}, u32[]{:S(2)}, u32[]{:S(2)}) collective-permute-start(f32[512,256]{1,0:T(8,128)S(1)} %pad_maximum_fusion.refs_4_), channel_id=1, source_target_pairs={{0,6},{1,7},{2,4},{3,5},{4,2},{5,3},{6,0},{7,1},{8,14},{9,15},{10,... | collective-permute-start | bytes 1572872 | tf_op jit(solution)/shard_map/ppermute | solution.py:198
  17.6 11.0 %collective-permute-start.17 = (f32[512,256]{1,0:T(8,128)S(1)}, f32[512,256]{1,0:T(8,128)S(1)}, u32[]{:S(2)}, u32[]{:S(2)}) collective-permute-start(f32[512,256]{1,0:T(8,128)S(1)} %collective-permute-done.14.refs_5_), channel_id=1, source_target_pairs={{8,16},{16,8},{9,17},{17,9},{10,18},{18,10},{11,19},{19,11},{12,20... | collective-permute-start | bytes 1572872 | tf_op jit(solution)/shard_map/ppermute | solution.py:207
  22.7 20.5 %collective-permute-start.16 = (f32[512,256]{1,0:T(8,128)S(1)}, f32[512,256]{1,0:T(8,128)S(1)}, u32[]{:S(2)}, u32[]{:S(2)}) collective-permute-start(f32[512,256]{1,0:T(8,128)S(1)} %collective-permute-done.15.refs_6_), channel_id=1, source_target_pairs={{8,0},{16,24},{9,1},{17,25},{10,2},{18,26},{11,3},{19,27},{12,4},{... | collective-permute-start | bytes 1572872 | tf_op jit(solution)/shard_map/ppermute | solution.py:208
  28.6 19.2 %collective-permute-start.18 = (f32[512,256]{1,0:T(8,128)S(1)}, f32[512,256]{1,0:T(8,128)S(1)}, u32[]{:S(2)}, u32[]{:S(2)}) collective-permute-start(f32[512,256]{1,0:T(8,128)S(1)} %collective-permute-done.17.refs_8_), channel_id=1, source_target_pairs={{8,0},{16,24},{9,1},{17,25},{10,2},{18,26},{11,3},{19,27},{12,4},{... | collective-permute-start | bytes 1572872 | tf_op jit(solution)/shard_map/ppermute | solution.py:209
  38.6 9.2 %copy-start.3 = (f32[512,256]{1,0:T(8,128)S(1)}, f32[512,256]{1,0:T(8,128)}, u32[]{:S(2)}) copy-start(f32[512,256]{1,0:T(8,128)} %refs_4_.1) | copy-start | bytes 1572868
  53.8 3.3 %copy-start.1 = (bf16[16,512,512]{2,1,0:T(8,128)(2,1)}, bf16[16,512,512]{2,1,0:T(8,128)(2,1)S(1)}, u32[]{:S(2)}) copy-start(bf16[16,512,512]{2,1,0:T(8,128)(2,1)S(1)} %get-tuple-element.101.refs_3_) | copy-start | bytes 25165828 | tf_op jit(solution)/shard_map/cond
  53.8 3.5 %copy-start.5 = (f32[512,256]{1,0:T(8,128)}, f32[512,256]{1,0:T(8,128)S(1)}, u32[]{:S(2)}) copy-start(f32[512,256]{1,0:T(8,128)S(1)} %get-tuple-element.107.refs_9_) | copy-start | bytes 1572868 | tf_op jit(solution)/shard_map/cond
  53.8 91.9 %collective-permute-start.1 = (f32[2,512,512]{2,1,0:T(8,128)}, f32[2,512,512]{2,1,0:T(8,128)}, u32[]{:S(2)}, u32[]{:S(2)}) collective-permute-start(f32[2,512,512]{2,1,0:T(8,128)} %get-tuple-element.97), channel_id=1, source_target_pairs={{0,16},{8,24},{16,0},{24,8},{1,17},{9,25},{17,1},{25,9},{2,18},{10... | collective-permute-start | bytes 6291464 | tf_op jit(solution)/shard_map/cond/branch_1_fun/ppermute | solution.py:198
  145.7 1.3 copy-start.7
  148.5 24.0 %collective-permute-start.9 = (f32[512,512]{1,0:T(8,128)S(1)}, f32[512,512]{1,0:T(8,128)}, u32[]{:S(2)}, u32[]{:S(2)}) collective-permute-start(f32[512,512]{1,0:T(8,128)S(1)} %param.9), channel_id=1, source_target_pairs={{0,7},{1,6},{2,5},{3,4},{4,3},{5,2},{6,1},{7,0},{8,15},{9,14},{10,... | collective-permute-start | bytes 3145736 | tf_op jit(solution)/shard_map/cond/branch_6_fun/ppermute | solution.py:198

commit v3 on v2

--- a/solution.py
+++ b/solution.py
@@ -132,8 +132,9 @@
 def right_kernel(given, block_rows, block_cols, shard_places, groups, *refs):
     me, row_partner, col_partner, w_ref = refs[:4]
     pieces = refs[4 : 4 + sum(groups)]
-    out, p_high, p_low = refs[4 + sum(groups) :]
+    first, second, p_high, p_low = refs[4 + sum(groups) :]
     step = pl.program_id(0)
+    steps = pl.num_programs(0)
     tile_order = w_ref.shape[2]
     depth = pieces[0].shape[0]
 
@@ -150,7 +151,15 @@
 
     _, block_col = place_of(given, block_rows, block_cols, me, row_partner, col_partner, step)
     rows = pl.ds(pl.multiple_of(block_col * tile_order, tile_order), tile_order)
-    out[0] = product(w_ref[0], p_high[rows, :], p_low[rows, :])
+    block = product(w_ref[0], p_high[rows, :], p_low[rows, :])
+
+    @pl.when(step < steps // 2)
+    def _():
+        first[...] = block
+
+    @pl.when(step >= steps // 2)
+    def _():
+        second[...] = block
 
 
 def right_products(given, tables, w, shards, shard_places, block_rows, block_cols):
@@ -167,10 +176,14 @@
         block_row, block_col = place(*refs, i)
         return block_row * block_cols + block_col, 0, 0
 
-    def out_at(i, *refs):
-        inside = i % per_quarter
-        return i // per_quarter, inside // half_cols, inside % half_cols
-
+    def out_spec(quarter):
+        def out_at(i, *refs):
+            inside = jnp.clip(i - quarter * per_quarter, 0, per_quarter - 1)
+            return inside // half_cols, inside % half_cols
+
+        return pl.BlockSpec((width, width), out_at)
+
+    out = jax.ShapeDtypeStruct((half_rows * width, half_cols * width), F32)
     whole = pl.BlockSpec((depth, width), lambda i, *_: (0, 0))
     return pl.pallas_call(
         functools.partial(
@@ -180,10 +193,10 @@
             num_scalar_prefetch=3,
             grid=(steps,),
             in_specs=[pl.BlockSpec((1, both, tile_order), w_at)] + [whole] * sum(groups),
-            out_specs=pl.BlockSpec((1, width, width), out_at),
+            out_specs=[out_spec(0), out_spec(1)],
             scratch_shapes=[pltpu.VMEM((len(shards) * depth, width), BF16)] * 2,
         ),
-        out_shape=jax.ShapeDtypeStruct((2, half_rows * width, half_cols * width), F32),
+        out_shape=[out, out],
         compiler_params=pltpu.CompilerParams(vmem_limit_bytes=VMEM_BYTES),
         cost_estimate=pl.CostEstimate(
             flops=12 * steps * width * width * tile_order,
@@ -206,7 +219,7 @@
     over = lax.ppermute(shard, axis, [(1, 2), (2, 1)])
     mate_over = lax.ppermute(mate, axis, [(1, 2), (2, 1)])
     handed = lax.ppermute(over, axis, [(1, 0), (2, 3)])
-    mate_handed = lax.ppermute(mate_over, axis, [(1, 0), (2, 3)])
+    mate_handed = lax.ppermute(mate, axis, [(2, 0), (1, 3)])
 
     def places(me):
         row = me[0]
@@ -255,18 +268,23 @@
         tables = (me, row_partner, col_partner)
         given = right_products(True, tables, w, shards, shard_places, block_rows, block_cols)
 
-        def row_branch(mask, given, w, shards):
-            received = flip(given, "row", n_row, mask)
+        def first_branch(mask, chunk, w, shards):
+            received = flip(chunk, "row", n_row, mask)
             kept = right_products(False, tables, w, shards, shard_places, block_rows, block_cols)
             return received, kept
 
-        def col_branch(mask, section):
-            return flip(section, "col", n_col, mask)
-
-        received, kept = pair_switch(row, row_partner[col, row], n_row, row_branch, given, w, shards)
-        section = kept[0] + received[0]
-        section = pair_switch(col, col_partner[row, col], n_col, col_branch, section)
-        return (kept[1] + received[1]) + section
+        def second_branch(mask, chunk):
+            return flip(chunk, "row", n_row, mask)
+
+        row_mate = row_partner[col, row]
+        col_mate = col_partner[row, col]
+        received, kept = pair_switch(row, row_mate, n_row, first_branch, given[0], w, shards)
+        section = kept[0] + received
+        sections = lax.all_gather(section, "col")
+        chunk, _ = lax.optimization_barrier((given[1], section))
+        received = pair_switch(row, row_mate, n_row, second_branch, chunk)
+        section = lax.dynamic_index_in_dim(sections, col_mate, 0, keepdims=False)
+        return (kept[1] + received) + section
 
     in_specs = (
         P(("row", "col"), None, None),

time: 179 us -> 186 us (1.039)
  between operations: 2.17 us -> 16.5 us
  waiting for transfers between devices: 118 us -> 107 us
  Pallas kernels: 31.8 us -> 38 us
  starting transfers between devices: 13.9 us -> 10.1 us
  local copies, waits for them, and re-layouts: 3.9 us -> 6.07 us
    ppermute x7, waiting for transfers between devices: 114 us -> 89.6 us  [flip(): return lax.ppermute(value, axis, [(i, i ^ mask) for i in range(size)])]
    all_gather x0 -> x1, waiting for transfers between devices: none -> 17.4 us  [body(): sections = lax.all_gather(section, 'col')]
    ppermute x1, waiting for transfers between devices: 4.64 us -> 0.01 us  [gather_prolong(): mate_handed = lax.ppermute(mate, axis, [(2, 0), (1, 3)])]
    pallas_call x4, Pallas kernels: 18 us -> 22.2 us  [left_products(): pl.pallas_call(functools.partial(left_kernel, block_of, block_cols, slot_...]
    ppermute x7, starting transfers between devices: 9.96 us -> 6.09 us  [flip(): return lax.ppermute(value, axis, [(i, i ^ mask) for i in range(size)])]
    pallas_call x2, Pallas kernels: 13.8 us -> 15.9 us  [right_products(): pl.pallas_call(functools.partial(right_kernel, given, block_rows, block_c...]
  transfers between devices with their start and end apart: 11 -> 12, of which waited for: 5 -> 4; matrix products, arithmetic and copies ran while one was open for 2% -> 2% of each run, Pallas kernels for 15% -> 17%
where the time goes in v3:
time: 186 us; the launch traced here: 184 us
  waiting for transfers between devices  107 us (58%)
  Pallas kernels  38 us (20%)
  between operations  16.5 us (9%)
  starting transfers between devices  10.1 us (5%)
  other arithmetic  6.36 us (3%)
  local copies, waits for them, and re-layouts  6.07 us (3%)
    ppermute x7, waiting for transfers between devices, flip(): return lax.ppermute(value, axis, [(i, i ^ mask) for i in range(size)])  89.6 us
    pallas_call x4, Pallas kernels, left_products(): pl.pallas_call(functools.partial(left_kernel, block_of, block_cols, slot_...  22.2 us
    all_gather x1, waiting for transfers between devices, body(): sections = lax.all_gather(section, 'col')  17.4 us
    pallas_call x2, Pallas kernels, right_products(): pl.pallas_call(functools.partial(right_kernel, given, block_rows, block_c...  15.9 us
    ppermute x7, starting transfers between devices, flip(): return lax.ppermute(value, axis, [(i, i ^ mask) for i in range(size)])  6.09 us
  transfers between devices with their start and end apart: 12, of which 4 were waited for; matrix products, arithmetic and copies ran while one was open for 2% of the time, Pallas kernels for 17%

profile of v3, /device:TPU:3, one launch (start us, length us, event | category | flops | bytes accessed | tf_op | source)
XLA Modules:
  0.0 184.1 jit_solution(13311330592989637387)
XLA Ops:
  6.5 0.7 collective-permute-start.6
  7.2 1.3 collective-permute-start.10
  8.5 0.7 collective-permute-start.11
  9.2 1.0 broadcast_select_fusion.1
  10.3 0.3 collective-permute-start.9
  10.6 0.8 copy.14.refs_1_
  12.0 0.8 copy.15.refs_1_
  12.7 1.2 dynamic_slice.10
  14.6 1.2 collective-permute-start.8
  15.9 1.2 collective-permute-start.7
  17.0 5.5 %left_products.4.refs_5_ = bf16[16,512,512]{2,1,0:T(8,128)(2,1)S(1)} custom-call(s32[2]{0:T(128)S(1)} %pad_add_fusion.refs_0_, s32[16,2]{1,0:T(8,128)S(1)} %copy.14.refs_1_, s32[1]{0:T(128)S(6)} %copy.34.refs_2_, f32[16,512,512]{2,1,0:T(8,128)} %refs_3_.7, f32[512,256]{1,0:T(8,128)S(1)} %pad_maximum_fusion.refs_4_), custom_call_target="tpu_custom_call" | custom-call | flops 3221225472 | bytes 6291456 | tf_op jit(solution)/shard_map/left_products/pallas_call | solution.py:91
  22.5 0.7 collective-permute-start.13
  23.2 1.3 collective-permute-start.14
  24.5 1.3 collective-permute-start.12
  25.8 5.6 %left_products.5.refs_5_ = bf16[16,512,512]{2,1,0:T(8,128)(2,1)S(1)} custom-call(s32[2]{0:T(128)S(1)} %pad_add_fusion.refs_0_, s32[16,2]{1,0:T(8,128)S(1)} %copy.14.refs_1_, s32[1]{0:T(128)S(6)} %copy.34.refs_2_, f32[16,512,512]{2,1,0:T(8,128)} %refs_3_.7, f32[512,256]{1,0:T(8,128)S(1)} %collective-permute-done.9.refs_4_, ...), custom_call_target="tpu_custom_call", output_to_operand_aliasing={{}: (5, {})} | custom-call | flops 3221225472 | bytes 6291456 | tf_op jit(solution)/shard_map/left_products/pallas_call | solution.py:91
  31.4 7.4 %collective-permute-done.8.refs_4_ = f32[512,256]{1,0:T(8,128)S(1)} collective-permute-done((f32[512,256]{1,0:T(8,128)S(1)}, f32[512,256]{1,0:T(8,128)S(1)}, u32[]{:S(2)}, u32[]{:S(2)}) %collective-permute-start.8) | collective-permute-done | bytes 524320 | tf_op jit(solution)/shard_map/ppermute | solution.py:211
  38.8 5.6 %left_products.6.refs_5_ = bf16[16,512,512]{2,1,0:T(8,128)(2,1)S(1)} custom-call(s32[2]{0:T(128)S(1)} %pad_add_fusion.refs_0_, s32[16,2]{1,0:T(8,128)S(1)} %copy.14.refs_1_, s32[1]{0:T(128)S(6)} %copy.34.refs_2_, f32[16,512,512]{2,1,0:T(8,128)} %refs_3_.7, f32[512,256]{1,0:T(8,128)S(1)} %collective-permute-done.8.refs_4_, ...), custom_call_target="tpu_custom_call", output_to_operand_aliasing={{}: (5, {})} | custom-call | flops 3221225472 | bytes 6291456 | tf_op jit(solution)/shard_map/left_products/pallas_call | solution.py:91
  44.4 5.6 %left_products.7.refs_3_ = bf16[16,512,512]{2,1,0:T(8,128)(2,1)S(1)} custom-call(s32[2]{0:T(128)S(1)} %pad_add_fusion.refs_0_, s32[16,2]{1,0:T(8,128)S(1)} %copy.14.refs_1_, s32[1]{0:T(128)S(6)} %copy.34.refs_2_, f32[16,512,512]{2,1,0:T(8,128)} %refs_3_.7, f32[512,256]{1,0:T(8,128)S(1)} %collective-permute-done.7.refs_4_, ...), custom_call_target="tpu_custom_call", output_to_operand_aliasing={{}: (5, {})} | custom-call | flops 3221225472 | bytes 6291456 | tf_op jit(solution)/shard_map/left_products/pallas_call | solution.py:91
  50.0 7.0 %right_products.7 = (f32[512,512]{1,0:T(8,128)}, f32[512,512]{1,0:T(8,128)S(1)}) custom-call(s32[2]{0:T(128)S(1)} %pad_add_fusion.refs_0_, s32[8,4]{1,0:T(8,128)S(1)} %copy.15.refs_1_, s32[4,8]{1,0:T(4,128)S(1)} %copy-done.4, bf16[16,512,512]{2,1,0:T(8,128)(2,1)S(1)} %left_products.7.refs_3_, f32[512,256]{1,0:T(8,128)} %refs_4_.1, ...), custom_call_target="tpu_custom_call" | custom-call | flops 3221225472 | bytes 6291456 | tf_op jit(solution)/shard_map/right_products/pallas_call | solution.py:188
  57.0 58.7 %conditional.2 = (f32[512,512]{1,0:T(8,128)}, f32[512,512]{1,0:T(8,128)S(1)}, f32[512,512]{1,0:T(8,128)S(1)}) conditional(s32[]{:T(128)} %clamp.4, (f32[512,512]{1,0:T(8,128)}, s32[2]{0:T(128)S(1)}, s32[8,4]{0,1:T(4,128)S(1)}, s32[4,8]{1,0:T(4,128)S(1)}, bf16[16,512,512]{2,1,0:T(8,128)(2,1)S(1)}, /*index=5*/f32[512,256]{1,0:T(8,128)}, ...), branch_computations={%region_0.1_spmd, %region_1.2_spmd, %region_2.3_spmd} | conditional | flops 3221225472 | bytes 54526440 | solution.py:235
  57.0 1.3 collective-permute-start.1
  58.4 1.9 %copy-done.1 = bf16[16,512,512]{2,1,0:T(8,128)(2,1)} copy-done((bf16[16,512,512]{2,1,0:T(8,128)(2,1)}, bf16[16,512,512]{2,1,0:T(8,128)(2,1)S(1)}, u32[]{:S(2)}) %copy-start.1) | copy-done | bytes 8388632 | tf_op jit(solution)/shard_map/cond
  60.5 0.2 copy-done.18
  60.9 0.2 copy-done.9
  61.1 8.9 %right_products.5 = (f32[512,512]{1,0:T(8,128)S(1)}, f32[512,512]{1,0:T(8,128)S(1)}) custom-call(s32[2]{0:T(128)S(1)} %get-tuple-element.92.refs_0_, s32[8,4]{1,0:T(8,128)S(1)} %copy.17.refs_1_, s32[4,8]{1,0:T(4,128)S(1)} %get-tuple-element.94.refs_2_, bf16[16,512,512]{2,1,0:T(8,128)(2,1)} %copy-done.1, f32[512,256]{1,0:T(8,128)} %get-tuple-element.96.refs_4_, ...), custom_call_target="tpu_custom_call" | custom-call | flops 3221225472 | bytes 6291456 | tf_op jit(solution)/shard_map/cond/branch_1_fun/right_products/pallas_call | solution.py:188
  70.0 45.7 %collective-permute-done.1 = f32[512,512]{1,0:T(8,128)} collective-permute-done((f32[512,512]{1,0:T(8,128)}, f32[512,512]{1,0:T(8,128)}, u32[]{:S(2)}, u32[]{:S(2)}) %collective-permute-start.1) | collective-permute-done | bytes 1048608 | tf_op jit(solution)/shard_map/cond/branch_1_fun/ppermute | solution.py:211
  115.7 2.4 %add.24 = f32[512,512]{1,0:T(8,128)} add(f32[512,512]{1,0:T(8,128)S(1)} %get-tuple-element.126, f32[512,512]{1,0:T(8,128)} %get-tuple-element.127) | non-fusion elementwise | flops 262144 | bytes 3145728 | tf_op jit(solution)/shard_map/add | solution.py:282
  118.1 0.6 dynamic_slice.11
  120.4 36.6 %conditional.3 = (f32[512,512]{1,0:T(8,128)}) conditional(s32[]{:T(128)} %clamp.4, f32[512,512]{1,0:T(8,128)S(1)} %get-tuple-element.128, f32[512,512]{1,0:T(8,128)S(1)} %get-tuple-element.128, f32[512,512]{1,0:T(8,128)S(1)} %get-tuple-element.128), branch_computations={%region_3.4_spmd, %region_4.5_spmd, %region_5.6_spmd} | conditional | bytes 4194352 | solution.py:235
  120.5 36.5 %collective-permute-done.4 = f32[512,512]{1,0:T(8,128)} collective-permute-done((f32[512,512]{1,0:T(8,128)S(1)}, f32[512,512]{1,0:T(8,128)}, u32[]{:S(2)}, u32[]{:S(2)}) %collective-permute-start.4) | collective-permute-done | bytes 1048608 | tf_op jit(solution)/shard_map/cond/branch_1_fun/ppermute | solution.py:211
  157.0 17.4 %all-gather.3.cloned.1.call-done = f32[4096,512]{1,0:T(8,128)} async-done(((f32[512,512]{1,0:T(8,128)}), f32[4096,512]{1,0:T(8,128)}) %all-gather.3.cloned.1.call-update) | async-done | bytes 8388624 | tf_op jit(solution)/shard_map/all_gather | solution.py:283
  174.4 2.9 %bitcast_add_fusion = f32[512,512]{1,0:T(8,128)} fusion(f32[8,512,512]{2,1,0:T(8,128)} %bitcast.7, s32[]{:T(128)S(6)} %select_n.29, f32[512,512]{1,0:T(8,128)S(1)} %get-tuple-element.124, f32[512,512]{1,0:T(8,128)} %get-tuple-element.173), kind=kLoop, calls=%fused_computation | loop fusion | flops 524288 | bytes 4194308 | tf_op jit(solution)/shard_map/add | solution.py:287
  (27 shorter events, 0.7 us)
Async XLA Ops:
  6.5 167.9 %all-gather.3.cloned.1.call-start = ((), (), s32[]{:S(2)}) async-start(), calls=%async_computation | async-start | bytes 9437184 | tf_op jit(solution)/shard_map/all_gather | solution.py:283
  6.5 2.7 %collective-permute-start.6 = (f32[256,256]{1,0:T(8,128)}, f32[256,256]{1,0:T(8,128)S(1)}, u32[]{:S(2)}, u32[]{:S(2)}) collective-permute-start(f32[256,256]{1,0:T(8,128)} %param.16), channel_id=1, source_target_pairs={{0,1},{1,0},{2,3},{3,2},{4,5},{5,4},{6,7},{7,6},{8,9},{9,8},{10,11... | collective-permute-start | bytes 786440 | tf_op jit(solution)/shard_map/ppermute | solution.py:211
  7.2 15.3 %collective-permute-start.10 = (f32[512,256]{1,0:T(8,128)}, f32[512,256]{1,0:T(8,128)S(1)}, u32[]{:S(2)}, u32[]{:S(2)}) collective-permute-start(f32[512,256]{1,0:T(8,128)} %refs_4_.1), channel_id=1, source_target_pairs={{0,8},{8,0},{16,24},{24,16},{1,9},{9,1},{17,25},{25,17},{2,10},{10... | collective-permute-start | bytes 1572872 | tf_op jit(solution)/shard_map/ppermute | solution.py:211
  8.5 14.7 %collective-permute-start.11 = (f32[512,256]{1,0:T(8,128)}, f32[512,256]{1,0:T(8,128)S(1)}, u32[]{:S(2)}, u32[]{:S(2)}) collective-permute-start(f32[512,256]{1,0:T(8,128)} %refs_4_.1), channel_id=1, source_target_pairs={{8,16},{16,8},{9,17},{17,9},{10,18},{18,10},{11,19},{19,11},{12,20... | collective-permute-start | bytes 1572872 | tf_op jit(solution)/shard_map/ppermute | solution.py:219
  10.3 14.2 %collective-permute-start.9 = (f32[512,256]{1,0:T(8,128)S(1)}, f32[512,256]{1,0:T(8,128)S(1)}, u32[]{:S(2)}, u32[]{:S(2)}) collective-permute-start(f32[512,256]{1,0:T(8,128)S(1)} %pad_maximum_fusion.refs_4_), channel_id=1, source_target_pairs={{0,2},{1,3},{2,0},{3,1},{4,6},{5,7},{6,4},{7,5},{8,10},{9,11},{10,... | collective-permute-start | bytes 1572872 | tf_op jit(solution)/shard_map/ppermute | solution.py:211
  14.6 24.2 %collective-permute-start.8 = (f32[512,256]{1,0:T(8,128)S(1)}, f32[512,256]{1,0:T(8,128)S(1)}, u32[]{:S(2)}, u32[]{:S(2)}) collective-permute-start(f32[512,256]{1,0:T(8,128)S(1)} %pad_maximum_fusion.refs_4_), channel_id=1, source_target_pairs={{0,4},{1,5},{2,6},{3,7},{4,0},{5,1},{6,2},{7,3},{8,12},{9,13},{10,... | collective-permute-start | bytes 1572872 | tf_op jit(solution)/shard_map/ppermute | solution.py:211
  15.9 28.5 %collective-permute-start.7 = (f32[512,256]{1,0:T(8,128)S(1)}, f32[512,256]{1,0:T(8,128)S(1)}, u32[]{:S(2)}, u32[]{:S(2)}) collective-permute-start(f32[512,256]{1,0:T(8,128)S(1)} %pad_maximum_fusion.refs_4_), channel_id=1, source_target_pairs={{0,6},{1,7},{2,4},{3,5},{4,2},{5,3},{6,0},{7,1},{8,14},{9,15},{10,... | collective-permute-start | bytes 1572872 | tf_op jit(solution)/shard_map/ppermute | solution.py:211
  22.5 27.5 %collective-permute-start.13 = (f32[512,256]{1,0:T(8,128)S(1)}, f32[512,256]{1,0:T(8,128)S(1)}, u32[]{:S(2)}, u32[]{:S(2)}) collective-permute-start(f32[512,256]{1,0:T(8,128)S(1)} %collective-permute-done.10.refs_5_), channel_id=1, source_target_pairs={{8,16},{16,8},{9,17},{17,9},{10,18},{18,10},{11,19},{19,11},{12,20... | collective-permute-start | bytes 1572872 | tf_op jit(solution)/shard_map/ppermute | solution.py:220
  23.2 26.8 %collective-permute-start.14 = (f32[512,256]{1,0:T(8,128)S(1)}, f32[512,256]{1,0:T(8,128)S(1)}, u32[]{:S(2)}, u32[]{:S(2)}) collective-permute-start(f32[512,256]{1,0:T(8,128)S(1)} %collective-permute-done.10.refs_5_), channel_id=1, source_target_pairs={{16,0},{8,24},{17,1},{9,25},{18,2},{10,26},{19,3},{11,27},{20,4},{... | collective-permute-start | bytes 1572872 | tf_op jit(solution)/shard_map/ppermute | solution.py:222
  24.5 25.5 %collective-permute-start.12 = (f32[512,256]{1,0:T(8,128)S(1)}, f32[512,256]{1,0:T(8,128)S(1)}, u32[]{:S(2)}, u32[]{:S(2)}) collective-permute-start(f32[512,256]{1,0:T(8,128)S(1)} %collective-permute-done.11.refs_6_), channel_id=1, source_target_pairs={{8,0},{16,24},{9,1},{17,25},{10,2},{18,26},{11,3},{19,27},{12,4},{... | collective-permute-start | bytes 1572872 | tf_op jit(solution)/shard_map/ppermute | solution.py:221
  44.3 5.7 %copy-start.4 = (s32[4,8]{1,0:T(4,128)S(1)}, s32[4,8]{1,0:T(4,128)}, u32[]{:S(2)}) copy-start(s32[4,8]{1,0:T(4,128)} %refs_2_.5) | copy-start | bytes 388
  49.9 7.0 %copy-start.3 = (s32[8,4]{0,1:T(4,128)S(1)}, s32[8,4]{0,1:T(4,128)}, u32[]{:S(2)}) copy-start(s32[8,4]{0,1:T(4,128)} %param.18) | copy-start | bytes 388
  57.0 3.3 %copy-start.1 = (bf16[16,512,512]{2,1,0:T(8,128)(2,1)}, bf16[16,512,512]{2,1,0:T(8,128)(2,1)S(1)}, u32[]{:S(2)}) copy-start(bf16[16,512,512]{2,1,0:T(8,128)(2,1)S(1)} %get-tuple-element.95.refs_3_) | copy-start | bytes 25165828 | tf_op jit(solution)/shard_map/cond
  57.0 3.4 %copy-start.12 = (f32[512,256]{1,0:T(8,128)}, f32[512,256]{1,0:T(8,128)S(1)}, u32[]{:S(2)}) copy-start(f32[512,256]{1,0:T(8,128)S(1)} %get-tuple-element.100.refs_8_) | copy-start | bytes 1572868 | tf_op jit(solution)/shard_map/cond
  57.0 3.5 %copy-start.15 = (f32[512,256]{1,0:T(8,128)}, f32[512,256]{1,0:T(8,128)S(1)}, u32[]{:S(2)}) copy-start(f32[512,256]{1,0:T(8,128)S(1)} %get-tuple-element.101.refs_9_) | copy-start | bytes 1572868 | tf_op jit(solution)/shard_map/cond
  57.0 3.7 %copy-start.18 = (f32[512,256]{1,0:T(8,128)}, f32[512,256]{1,0:T(8,128)S(1)}, u32[]{:S(2)}) copy-start(f32[512,256]{1,0:T(8,128)S(1)} %get-tuple-element.99.refs_7_) | copy-start | bytes 1572868 | tf_op jit(solution)/shard_map/cond
  57.0 3.9 %copy-start.6 = (f32[512,256]{1,0:T(8,128)}, f32[512,256]{1,0:T(8,128)S(1)}, u32[]{:S(2)}) copy-start(f32[512,256]{1,0:T(8,128)S(1)} %get-tuple-element.97.refs_5_) | copy-start | bytes 1572868 | tf_op jit(solution)/shard_map/cond
  57.0 4.0 %copy-start.9 = (f32[512,256]{1,0:T(8,128)}, f32[512,256]{1,0:T(8,128)S(1)}, u32[]{:S(2)}) copy-start(f32[512,256]{1,0:T(8,128)S(1)} %get-tuple-element.98.refs_6_) | copy-start | bytes 1572868 | tf_op jit(solution)/shard_map/cond
  57.0 58.7 %collective-permute-start.1 = (f32[512,512]{1,0:T(8,128)}, f32[512,512]{1,0:T(8,128)}, u32[]{:S(2)}, u32[]{:S(2)}) collective-permute-start(f32[512,512]{1,0:T(8,128)} %get-tuple-element.91), channel_id=1, source_target_pairs={{0,16},{8,24},{16,0},{24,8},{1,17},{9,25},{17,1},{25,9},{2,18},{10... | collective-permute-start | bytes 3145736 | tf_op jit(solution)/shard_map/cond/branch_1_fun/ppermute | solution.py:211
  120.5 36.6 %collective-permute-start.4 = (f32[512,512]{1,0:T(8,128)S(1)}, f32[512,512]{1,0:T(8,128)}, u32[]{:S(2)}, u32[]{:S(2)}) collective-permute-start(f32[512,512]{1,0:T(8,128)S(1)} %param.4), channel_id=1, source_target_pairs={{0,16},{8,24},{16,0},{24,8},{1,17},{9,25},{17,1},{25,9},{2,18},{10... | collective-permute-start | bytes 3145736 | tf_op jit(solution)/shard_map/cond/branch_1_fun/ppermute | solution.py:211
Sparse Core Ops, SparseCore 0:
  118.2 56.1 all-gather.2

commit v4 on v3

--- a/solution.py
+++ b/solution.py
@@ -29,29 +29,31 @@
     return over_high[:half] + (over_high[half:] + over_low)
 
 
-def slot_at(coords, place, block_cols, slot_count):
-    found = jnp.int32(-1)
-    for slot in range(slot_count):
-        hit = coords[slot, 0] * block_cols + coords[slot, 1] == place
-        found = jnp.where(hit, jnp.int32(slot), found)
-    return found
-
-
-def left_kernel(block_of, block_cols, slot_count, *refs):
-    me, coords, counts, tile_ref, q_ref = refs[:5]
+def div(value, by):
+    return lax.div(value, jnp.int32(by))
+
+
+def rem(value, by):
+    return lax.rem(value, jnp.int32(by))
+
+
+def left_kernel(row_of, load, block_cols, half_rows, *refs):
+    me, slots, row_partner, tile_ref = refs[:4]
+    q_refs = refs[4 : 4 + load.count]
     out, q_both = refs[-2:]
     group, column = pl.program_id(0), pl.program_id(1)
     width = q_both.shape[0] // 2
 
     @pl.when(column == 0)
     def _():
-        high, low = split(q_ref[...].T)
-        q_both[:width] = high
-        q_both[width:] = low
-
-    place = block_of(me, group) * block_cols + column
-    slot = slot_at(coords, place, block_cols, slot_count)
-    live = (slot >= 0) & (slot < counts[0])
+        def put(value, first):
+            high, low = split(value.T)
+            q_both[:width, first : first + value.shape[0]] = high
+            q_both[width:, first : first + value.shape[0]] = low
+
+        load(me, row_partner, group, q_refs, put)
+
+    live = slots[row_of(me, row_partner, group) * block_cols + column] >= 0
 
     @pl.when(live)
     def _():
@@ -65,31 +67,25 @@
         out[...] = jnp.zeros_like(out)
 
 
-def left_products(me, coords, counts, tiles, q_rows, block_of, block_rows, block_cols, before):
-    slot_count, tile_order, _ = tiles.shape
-    width = q_rows.shape[1]
-    groups = q_rows.shape[0] // tile_order
-    positions = block_rows * block_cols
-
-    def tile_at(g, b, me_ref, coords_ref, counts_ref):
-        place = block_of(me_ref, g) * block_cols + b
-        return jnp.maximum(slot_at(coords_ref, place, block_cols, slot_count), 0), 0, 0
-
-    def out_at(g, b, me_ref, coords_ref, counts_ref):
-        return block_of(me_ref, g) * block_cols + b, 0, 0
-
-    in_specs = [
-        pl.BlockSpec((1, tile_order, tile_order), tile_at),
-        pl.BlockSpec((tile_order, width), lambda g, b, *_: (g, 0)),
-    ]
-    operands = [me, coords, counts, tiles, q_rows]
+def left_products(tables, tiles, q_pieces, q_specs, row_of, load, groups, half_rows, block_cols, before):
+    _, tile_order, _ = tiles.shape
+    width = q_pieces[0].shape[1]
+
+    def tile_at(g, b, me, slots, row_partner):
+        return jnp.maximum(slots[row_of(me, row_partner, g) * block_cols + b], 0), 0, 0
+
+    def out_at(g, b, me, slots, row_partner):
+        return rem(row_of(me, row_partner, g), half_rows) * block_cols + b, 0, 0
+
+    in_specs = [pl.BlockSpec((1, tile_order, tile_order), tile_at)] + q_specs
+    operands = [*tables, tiles, *q_pieces]
     aliases = {}
     if before is not None:
         in_specs.append(pl.BlockSpec(memory_space=pl.ANY))
         aliases = {len(operands): 0}
         operands.append(before)
     return pl.pallas_call(
-        functools.partial(left_kernel, block_of, block_cols, slot_count),
+        functools.partial(left_kernel, row_of, load, block_cols, half_rows),
         grid_spec=pltpu.PrefetchScalarGridSpec(
             num_scalar_prefetch=3,
             grid=(groups, block_cols),
@@ -97,7 +93,7 @@
             out_specs=pl.BlockSpec((1, 2 * width, tile_order), out_at),
             scratch_shapes=[pltpu.VMEM((2 * width, tile_order), BF16)],
         ),
-        out_shape=jax.ShapeDtypeStruct((positions, 2 * width, tile_order), BF16),
+        out_shape=jax.ShapeDtypeStruct((half_rows * block_cols, 2 * width, tile_order), BF16),
         input_output_aliases=aliases,
         compiler_params=pltpu.CompilerParams(vmem_limit_bytes=VMEM_BYTES),
         cost_estimate=pl.CostEstimate(
@@ -109,6 +105,60 @@
     )(*operands)
 
 
+def half_of(given, me, row_partner):
+    mate = row_partner[me[1], me[0]]
+    return ((mate > me[0]) if given else (me[0] > mate)).astype(jnp.int32)
+
+
+class ChipBlocks:
+    def __init__(self, given, pairs):
+        self.given = given
+        self.pairs = pairs
+        self.count = 4 * len(pairs)
+
+    def pick(self, me, row_partner):
+        chip = div(me[1], 2)
+        return half_of(self.given, me, row_partner) == div(chip, 2)
+
+    def row_of(self, me, row_partner, group):
+        near_half = self.pick(me, row_partner)
+        row = jnp.int32(0)
+        for index, (near, far) in enumerate(self.pairs):
+            chip = div(me[1], 2) ^ jnp.where(near_half, near, far)
+            row = jnp.where(group == index, chip, row)
+        return row
+
+    def __call__(self, me, row_partner, group, refs, put):
+        near_half = self.pick(me, row_partner)
+        odd = rem(me[1], 2) == 1
+        for index in range(len(self.pairs)):
+            for far in range(2):
+                for swap in range(2):
+                    first, second = refs[4 * index + 2 * far : 4 * index + 2 * far + 2]
+                    wanted = near_half if far == 0 else jnp.logical_not(near_half)
+                    order = odd if swap == 1 else jnp.logical_not(odd)
+
+                    @pl.when((group == index) & wanted & order)
+                    def _():
+                        depth = first.shape[0]
+                        put(first[...], swap * depth)
+                        put(second[...], (1 - swap) * depth)
+
+
+class WholeBlocks:
+    count = 1
+
+    def __init__(self, given, half_rows):
+        self.given = given
+        self.half_rows = half_rows
+
+    def row_of(self, me, row_partner, group):
+        return half_of(self.given, me, row_partner) * self.half_rows + group
+
+    def __call__(self, me, row_partner, group, refs, put):
+        put(refs[0][...], 0)
+
+
 def mates(me, row_partner, col_partner):
     row, col = me[0], me[1]
     row_mate = row_partner[col, row]
@@ -116,17 +166,12 @@
 
 
 def place_of(given, block_rows, block_cols, me, row_partner, col_partner, step):
-    row, col, row_mate, col_mate, row_mates_col = mates(me, row_partner, col_partner)
+    row, col, _, col_mate, row_mates_col = mates(me, row_partner, col_partner)
     half_rows, half_cols = block_rows // 2, block_cols // 2
-    quarter, inside = step // (half_rows * half_cols), step % (half_rows * half_cols)
-    if given:
-        row_half, keeps = row_mate > row, col > row_mates_col
-    else:
-        row_half, keeps = row > row_mate, col > col_mate
+    quarter, inside = div(step, half_rows * half_cols), rem(step, half_rows * half_cols)
+    keeps = col > (row_mates_col if given else col_mate)
     col_half = jnp.where(keeps, quarter, 1 - quarter)
-    block_row = jnp.where(row_half, half_rows, 0) + inside // half_cols
-    block_col = col_half * half_cols + inside % half_cols
-    return block_row, block_col
+    return div(inside, half_cols), col_half * half_cols + rem(inside, half_cols)
 
 
 def right_kernel(given, block_rows, block_cols, shard_places, groups, *refs):
@@ -179,7 +224,7 @@
     def out_spec(quarter):
         def out_at(i, *refs):
             inside = jnp.clip(i - quarter * per_quarter, 0, per_quarter - 1)
-            return inside // half_cols, inside % half_cols
+            return div(inside, half_cols), rem(inside, half_cols)
 
         return pl.BlockSpec((width, width), out_at)
 
@@ -248,42 +293,85 @@
         col = lax.axis_index("col").astype(jnp.int32)
         me = jnp.stack([row, col])
 
+        half_rows, half_cols = block_rows // 2, block_cols // 2
+
         shards, shard_places = gather_prolong(prolong, "row", n_row)
-
-        left = functools.partial(left_products, me, coords, counts, tiles)
-        if n_col == 8 and tile_order == 2 * q_depth:
-            mate = flip(restrict, "col", n_col, 1)
-            odd = (col & 1) == 1
-            own = jnp.concatenate(
-                [jnp.where(odd, mate, restrict), jnp.where(odd, restrict, mate)], axis=0
+        by_chip = n_col == 8 and block_rows == 4 and tile_order == 2 * q_depth
+        if by_chip:
+            q_pieces = [restrict] + [flip(restrict, "col", n_col, m) for m in range(1, n_col)]
+        else:
+            q_pieces = [lax.all_gather(restrict, "col", axis=0, tiled=True)]
+
+        slot_ids = jnp.arange(tiles.shape[0], dtype=jnp.int32)
+        place_ids = jnp.arange(block_rows * block_cols, dtype=jnp.int32)
+        named = (coords[:, 0] * block_cols + coords[:, 1])[None, :] == place_ids[:, None]
+        hit = named & (slot_ids < counts[0])[None, :]
+        slots = jnp.max(jnp.where(hit, slot_ids[None, :], -1), axis=1)
+
+        def left(given, pairs, before=None):
+            tables = (me, slots, row_partner)
+            if by_chip:
+                load = ChipBlocks(given, pairs)
+                pieces = [
+                    q_pieces[2 * chip + core] for pair in pairs for chip in pair for core in range(2)
+                ]
+                specs = [pl.BlockSpec(restrict.shape, lambda g, b, *_: (0, 0))] * len(pieces)
+                groups = len(pairs)
+            else:
+                load = WholeBlocks(given, half_rows)
+                pieces = q_pieces
+                specs = [
+                    pl.BlockSpec(
+                        (tile_order, restrict.shape[1]),
+                        lambda g, b, me, slots, row_partner: (load.row_of(me, row_partner, g), 0),
+                    )
+                ]
+                groups = half_rows
+            return left_products(
+                tables, tiles, pieces, specs, load.row_of, load, groups, half_rows, block_cols, before
             )
-            w = None
-            for chip in range(n_col // 2):
-                block = own if chip == 0 else flip(own, "col", n_col, 2 * chip)
-                w = left(block, lambda ref, g, chip=chip: (ref[1] // 2) ^ chip, block_rows, block_cols, w)
+
+        def right(given, w):
+            tables = (me, row_partner, col_partner)
+            return right_products(given, tables, w, shards, shard_places, block_rows, block_cols)
+
+        if by_chip:
+            given = right(True, left(True, [(1, 3)], left(True, [(0, 2)])))
         else:
-            blocks = lax.all_gather(restrict, "col", axis=0, tiled=True)
-            w = left(blocks, lambda ref, g: g, block_rows, block_cols, None)
-
-        tables = (me, row_partner, col_partner)
-        given = right_products(True, tables, w, shards, shard_places, block_rows, block_cols)
-
-        def first_branch(mask, chunk, w, shards):
+            given = right(True, left(True, None))
+
+        def first_branch(mask, chunk):
             received = flip(chunk, "row", n_row, mask)
-            kept = right_products(False, tables, w, shards, shard_places, block_rows, block_cols)
-            return received, kept
+            return received, right(False, left(False, [(0, 2), (1, 3)]))
 
         def second_branch(mask, chunk):
             return flip(chunk, "row", n_row, mask)
 
         row_mate = row_partner[col, row]
         col_mate = col_partner[row, col]
-        received, kept = pair_switch(row, row_mate, n_row, first_branch, given[0], w, shards)
+        received, kept = pair_switch(row, row_mate, n_row, first_branch, given[0])
         section = kept[0] + received
-        sections = lax.all_gather(section, "col")
-        chunk, _ = lax.optimization_barrier((given[1], section))
+        chunk, section = lax.optimization_barrier((given[1], section))
+        if n_col == 8:
+            over = [section] + [flip(section, "col", n_col, 2 * chip) for chip in range(1, 4)]
+        else:
+            over = lax.all_gather(section, "col")
         received = pair_switch(row, row_mate, n_row, second_branch, chunk)
-        section = lax.dynamic_index_in_dim(sections, col_mate, 0, keepdims=False)
+        over, received = lax.optimization_barrier((over, received))
+        if n_col == 8:
+            def pick(distance):
+                chip = distance >> 1
+                return jnp.where(
+                    chip < 2,
+                    jnp.where(chip == 0, over[0], over[1]),
+                    jnp.where(chip == 2, over[2], over[3]),
+                )
+
+            handed = flip(pick(col ^ 1 ^ col_partner[row, col ^ 1]), "col", n_col, 1)
+            distance = col ^ col_mate
+            section = jnp.where((distance & 1) == 1, handed, pick(distance))
+        else:
+            section = lax.dynamic_index_in_dim(over, col_mate, 0, keepdims=False)
         return (kept[1] + received) + section
 
     in_specs = (

time: 186 us -> 172 us (0.925)
  the two profiles are of different devices: /device:TPU:3 before, /device:TPU:9 now
where the time goes in v4:
time: 172 us
  waiting for transfers between devices  100 us (58%)
  starting transfers between devices  30.1 us (18%)
  Pallas kernels  28 us (16%)
  other arithmetic  7.61 us (4%)
  local copies, waits for them, and re-layouts  2.82 us (2%)
  between operations  2.71 us (2%)
    ppermute x14, waiting for transfers between devices, flip(): return lax.ppermute(value, axis, [(i, i ^ mask) for i in range(size)])  89.9 us
    ppermute x14, starting transfers between devices, flip(): return lax.ppermute(value, axis, [(i, i ^ mask) for i in range(size)])  21.1 us
    pallas_call x3, Pallas kernels, left_products(): pl.pallas_call(functools.partial(left_kernel, row_of, load, block_cols, h...  15.2 us
    pallas_call x2, Pallas kernels, right_products(): pl.pallas_call(functools.partial(right_kernel, given, block_rows, block_c...  12.7 us
    ppermute x1, waiting for transfers between devices, gather_prolong(): mate_handed = lax.ppermute(mate, axis, [(2, 0), (1, 3)])  5.81 us
    ppermute x1, waiting for transfers between devices, gather_prolong(): handed = lax.ppermute(over, axis, [(1, 0), (2, 3)])  4.68 us
    ppermute x1, starting transfers between devices, gather_prolong(): over = lax.ppermute(shard, axis, [(1, 2), (2, 1)])  4.49 us
    add x1, other arithmetic, body(): return kept[1] + received + section  3.73 us
  transfers between devices with their start and end apart: 18, of which 9 were waited for; matrix products, arithmetic and copies ran while one was open for 2% of the time, Pallas kernels for 12%

profile of v4, /device:TPU:9, one launch (start us, length us, event | category | flops | bytes accessed | tf_op | source)
XLA Modules:
  0.0 171.8 jit_solution(10077167466324950941)
XLA Ops:
  0.7 1.2 collective-permute-start.11
  2.3 4.5 %collective-permute-start.14 = (f32[512,256]{1,0:T(8,128)}, f32[512,256]{1,0:T(8,128)S(1)}, u32[]{:S(2)}, u32[]{:S(2)}) collective-permute-start(f32[512,256]{1,0:T(8,128)} %refs_4_.3), channel_id=1, source_target_pairs={{8,16},{16,8},{9,17},{17,9},{10,18},{18,10},{11,19},{19,11},{12,20... | collective-permute-start | bytes 1572872 | tf_op jit(solution)/shard_map/ppermute | solution.py:264
  8.2 1.2 collective-permute-start.6
  9.4 1.7 collective-permute-start.7
  11.9 1.3 dynamic_slice.9
  14.8 2.2 %collective-permute-start.8 = (f32[256,256]{1,0:T(8,128)}, f32[256,256]{1,0:T(8,128)S(1)}, u32[]{:S(2)}, u32[]{:S(2)}) collective-permute-start(f32[256,256]{1,0:T(8,128)} %refs_4_.2), channel_id=1, source_target_pairs={{0,6},{1,7},{2,4},{3,5},{4,2},{5,3},{6,0},{7,1},{8,14},{9,15},{10,... | collective-permute-start | bytes 786440 | tf_op jit(solution)/shard_map/ppermute | solution.py:256
  17.0 3.5 %collective-permute-start.9 = (f32[256,256]{1,0:T(8,128)}, f32[256,256]{1,0:T(8,128)S(1)}, u32[]{:S(2)}, u32[]{:S(2)}) collective-permute-start(f32[256,256]{1,0:T(8,128)} %refs_4_.2), channel_id=1, source_target_pairs={{0,7},{1,6},{2,5},{3,4},{4,3},{5,2},{6,1},{7,0},{8,15},{9,14},{10,... | collective-permute-start | bytes 786440 | tf_op jit(solution)/shard_map/ppermute | solution.py:256
  20.5 1.9 %collective-permute-start.16 = (f32[512,256]{1,0:T(8,128)S(1)}, f32[512,256]{1,0:T(8,128)S(1)}, u32[]{:S(2)}, u32[]{:S(2)}) collective-permute-start(f32[512,256]{1,0:T(8,128)S(1)} %collective-permute-done.13.refs_5_), channel_id=1, source_target_pairs={{8,16},{16,8},{9,17},{17,9},{10,18},{18,10},{11,19},{19,11},{12,20... | collective-permute-start | bytes 1572872 | tf_op jit(solution)/shard_map/ppermute | solution.py:265
  22.4 1.2 collective-permute-done.7.refs_5_
  23.7 1.3 collective-permute-start.17
  25.0 1.3 collective-permute-start.15
  26.3 4.7 %left_products.8.refs_8_ = bf16[8,512,512]{2,1,0:T(8,128)(2,1)S(1)} custom-call(s32[2]{0:T(128)S(1)} %pad_add_fusion.refs_0_, s32[16]{0:T(128)S(1)} %select_reduce_fusion.refs_1_, s32[8,4]{1,0:T(8,128)S(1)} %copy.17.refs_2_.refs_1_, f32[16,512,512]{2,1,0:T(8,128)} %refs_3_.3, f32[256,256]{1,0:T(8,128)} %refs_4_.2, ...), custom_call_target="tpu_custom_call" | custom-call | flops 3221225472 | bytes 6291456 | tf_op jit(solution)/shard_map/left_products/pallas_call | solution.py:87
  31.1 3.2 %collective-permute-done.9.refs_7_ = f32[256,256]{1,0:T(8,128)S(1)} collective-permute-done((f32[256,256]{1,0:T(8,128)}, f32[256,256]{1,0:T(8,128)S(1)}, u32[]{:S(2)}, u32[]{:S(2)}) %collective-permute-start.9) | collective-permute-done | bytes 262176 | tf_op jit(solution)/shard_map/ppermute | solution.py:256
  34.3 4.1 %left_products.9.refs_3_ = bf16[8,512,512]{2,1,0:T(8,128)(2,1)S(1)} custom-call(s32[2]{0:T(128)S(1)} %pad_add_fusion.refs_0_, s32[16]{0:T(128)S(1)} %select_reduce_fusion.refs_1_, s32[8,4]{1,0:T(8,128)S(1)} %copy.17.refs_2_.refs_1_, f32[16,512,512]{2,1,0:T(8,128)} %refs_3_.3, ...), custom_call_target="tpu_custom_call", output_to_operand_aliasing={{}: (8, {})} | custom-call | flops 3221225472 | bytes 6291456 | tf_op jit(solution)/shard_map/left_products/pallas_call | solution.py:87
  38.5 5.8 %collective-permute-done.17.refs_9_ = f32[512,256]{1,0:T(8,128)S(1)} collective-permute-done((f32[512,256]{1,0:T(8,128)S(1)}, f32[512,256]{1,0:T(8,128)S(1)}, u32[]{:S(2)}, u32[]{:S(2)}) %collective-permute-start.17) | collective-permute-done | bytes 524320 | tf_op jit(solution)/shard_map/ppermute | solution.py:267
  44.3 4.7 %collective-permute-done.15.refs_7_ = f32[512,256]{1,0:T(8,128)S(1)} collective-permute-done((f32[512,256]{1,0:T(8,128)S(1)}, f32[512,256]{1,0:T(8,128)S(1)}, u32[]{:S(2)}, u32[]{:S(2)}) %collective-permute-start.15) | collective-permute-done | bytes 524320 | tf_op jit(solution)/shard_map/ppermute | solution.py:266
  48.9 7.1 %right_products.7 = (f32[512,512]{1,0:T(8,128)S(1)}, f32[512,512]{1,0:T(8,128)}) custom-call(s32[2]{0:T(128)S(1)} %pad_add_fusion.refs_0_, s32[8,4]{1,0:T(8,128)S(1)} %copy.17.refs_2_.refs_1_, s32[4,8]{1,0:T(4,128)S(1)} %copy-done.2, bf16[8,512,512]{2,1,0:T(8,128)(2,1)S(1)} %left_products.9.refs_3_, f32[512,256]{1,0:T(8,128)} %refs_4_.3, ...), custom_call_target="tpu_custom_call" | custom-call | flops 3221225472 | bytes 6291456 | tf_op jit(solution)/shard_map/right_products/pallas_call | solution.py:233
  56.0 57.0 %conditional.2 = (f32[512,512]{1,0:T(8,128)}, f32[512,512]{1,0:T(8,128)S(1)}, f32[512,512]{1,0:T(8,128)}) conditional(s32[]{:T(128)} %clamp.4, (f32[512,512]{1,0:T(8,128)S(1)}, s32[2]{0:T(128)S(1)}, s32[16]{0:T(128)S(1)}, s32[8,4]{0,1:T(4,128)S(1)}, f32[16,512,512]{2,1,0:T(8,128)}, /*index=5*/f32[256,256]{1,0:T(8,128)S(1)}, ...), branch_computations={%region_1.2_spmd, %region_2.3_spmd, %region_3.4_spmd} | conditional | flops 9663676416 | bytes 41943612 | solution.py:280
  56.0 1.4 collective-permute-start.1
  57.5 6.4 %left_products.6.refs_3_ = bf16[8,512,512]{2,1,0:T(8,128)(2,1)S(1)} custom-call(s32[2]{0:T(128)S(1)} %get-tuple-element.155.refs_0_, s32[16]{0:T(128)S(1)} %get-tuple-element.158.refs_1_, s32[8,4]{1,0:T(8,128)S(1)} %copy.19.refs_2_.refs_1_, f32[16,512,512]{2,1,0:T(8,128)} %get-tuple-element.159.refs_3_, f32[256,256]{1,0:T(8,128)S(1)} %get-tuple-element.160.refs_4_, ...), custom_call_target="tpu_custom_call" | custom-call | flops 6442450944 | bytes 12582912 | tf_op jit(solution)/shard_map/cond/branch_1_fun/left_products/pallas_call | solution.py:87
  64.0 5.7 %right_products.5 = (f32[512,512]{1,0:T(8,128)S(1)}, f32[512,512]{1,0:T(8,128)}) custom-call(s32[2]{0:T(128)S(1)} %get-tuple-element.155.refs_0_, s32[8,4]{1,0:T(8,128)S(1)} %copy.19.refs_2_.refs_1_, s32[4,8]{1,0:T(4,128)S(1)} %get-tuple-element.157.refs_2_, bf16[8,512,512]{2,1,0:T(8,128)(2,1)S(1)} %left_products.6.refs_3_, f32[512,256]{1,0:T(8,128)S(1)} %copy-done.4, ...), custom_call_target="tpu_custom_call" | custom-call | flops 3221225472 | bytes 6291456 | tf_op jit(solution)/shard_map/cond/branch_1_fun/right_products/pallas_call | solution.py:233
  69.7 43.4 %collective-permute-done.1 = f32[512,512]{1,0:T(8,128)} collective-permute-done((f32[512,512]{1,0:T(8,128)S(1)}, f32[512,512]{1,0:T(8,128)}, u32[]{:S(2)}, u32[]{:S(2)}) %collective-permute-start.1) | collective-permute-done | bytes 1048608 | tf_op jit(solution)/shard_map/cond/branch_1_fun/ppermute | solution.py:256
  113.1 1.4 add.36
  114.7 2.6 %collective-permute-start.20 = (f32[512,512]{1,0:T(8,128)S(1)}, f32[512,512]{1,0:T(8,128)}, u32[]{:S(2)}, u32[]{:S(2)}) collective-permute-start(f32[512,512]{1,0:T(8,128)S(1)} %add.36), channel_id=1, source_target_pairs={{0,6},{1,7},{2,4},{3,5},{4,2},{5,3},{6,0},{7,1},{8,14},{9,15},{10,... | collective-permute-start | bytes 3145736 | tf_op jit(solution)/shard_map/ppermute | solution.py:256
  118.6 37.5 %conditional.3 = (f32[512,512]{1,0:T(8,128)}) conditional(s32[]{:T(128)} %clamp.4, f32[512,512]{1,0:T(8,128)} %get-tuple-element.216, f32[512,512]{1,0:T(8,128)} %get-tuple-element.216, f32[512,512]{1,0:T(8,128)} %get-tuple-element.216), branch_computations={%region_4.5_spmd, %region_5.6_spmd, %region_6.7_spmd} | conditional | bytes 4194352 | solution.py:280
  118.6 3.3 %collective-permute-start.4 = (f32[512,512]{1,0:T(8,128)}, f32[512,512]{1,0:T(8,128)}, u32[]{:S(2)}, u32[]{:S(2)}) collective-permute-start(f32[512,512]{1,0:T(8,128)} %param.4), channel_id=1, source_target_pairs={{0,16},{8,24},{16,0},{24,8},{1,17},{9,25},{17,1},{25,9},{2,18},{10... | collective-permute-start | bytes 3145736 | tf_op jit(solution)/shard_map/cond/branch_1_fun/ppermute | solution.py:256
  121.9 34.2 %collective-permute-done.4 = f32[512,512]{1,0:T(8,128)} collective-permute-done((f32[512,512]{1,0:T(8,128)}, f32[512,512]{1,0:T(8,128)}, u32[]{:S(2)}, u32[]{:S(2)}) %collective-permute-start.4) | collective-permute-done | bytes 1048608 | tf_op jit(solution)/shard_map/cond/branch_1_fun/ppermute | solution.py:256
  156.1 4.9 %collective-permute-done.19 = f32[512,512]{1,0:T(8,128)S(1)} collective-permute-done((f32[512,512]{1,0:T(8,128)S(1)}, f32[512,512]{1,0:T(8,128)S(1)}, u32[]{:S(2)}, u32[]{:S(2)}) %collective-permute-start.19) | collective-permute-done | bytes 1048608 | tf_op jit(solution)/shard_map/ppermute | solution.py:256
  161.0 1.5 select_select_fusion
  162.5 2.9 %collective-permute-start.21 = (f32[512,512]{1,0:T(8,128)}, f32[512,512]{1,0:T(8,128)}, u32[]{:S(2)}, u32[]{:S(2)}) collective-permute-start(f32[512,512]{1,0:T(8,128)} %select_select_fusion), channel_id=1, source_target_pairs={{0,1},{1,0},{2,3},{3,2},{4,5},{5,4},{6,7},{7,6},{8,9},{9,8},{10,11... | collective-permute-start | bytes 3145736 | tf_op jit(solution)/shard_map/ppermute | solution.py:256
  166.0 2.0 %collective-permute-done.21 = f32[512,512]{1,0:T(8,128)} collective-permute-done((f32[512,512]{1,0:T(8,128)}, f32[512,512]{1,0:T(8,128)}, u32[]{:S(2)}, u32[]{:S(2)}) %collective-permute-start.21) | collective-permute-done | bytes 1048608 | tf_op jit(solution)/shard_map/ppermute | solution.py:256
  168.0 3.7 %select_add_fusion = f32[512,512]{1,0:T(8,128)} fusion(f32[512,512]{1,0:T(8,128)} %collective-permute-done.21, f32[512,512]{1,0:T(8,128)S(1)} %collective-permute-done.19, f32[512,512]{1,0:T(8,128)} %collective-permute-done.20, f32[512,512]{1,0:T(8,128)S(1)} %add.36, f32[512,512]{1,0:T(8,128)S(1)} %collective-permute-done.18, ...), kind=kLoop, calls=%fused_computation | loop fusion | flops 1572864 | bytes 8388612 | tf_op jit(solution)/shard_map/add | solution.py:375
  (50 shorter events, 4.7 us)
Async XLA Ops:
  0.0 8.2 %collective-permute-start.10 = (f32[256,256]{1,0:T(8,128)}, f32[256,256]{1,0:T(8,128)S(1)}, u32[]{:S(2)}, u32[]{:S(2)}) collective-permute-start(f32[256,256]{1,0:T(8,128)} %refs_4_.2), channel_id=1, source_target_pairs={{0,1},{1,0},{2,3},{3,2},{4,5},{5,4},{6,7},{7,6},{8,9},{9,8},{10,11... | collective-permute-start | bytes 786440 | tf_op jit(solution)/shard_map/ppermute | solution.py:256
  0.7 8.8 %collective-permute-start.11 = (f32[256,256]{1,0:T(8,128)}, f32[256,256]{1,0:T(8,128)S(1)}, u32[]{:S(2)}, u32[]{:S(2)}) collective-permute-start(f32[256,256]{1,0:T(8,128)} %refs_4_.2), channel_id=1, source_target_pairs={{0,4},{1,5},{2,6},{3,7},{4,0},{5,1},{6,2},{7,3},{8,12},{9,13},{10,... | collective-permute-start | bytes 786440 | tf_op jit(solution)/shard_map/ppermute | solution.py:256
  1.9 12.9 %collective-permute-start.12 = (f32[256,256]{1,0:T(8,128)}, f32[256,256]{1,0:T(8,128)S(1)}, u32[]{:S(2)}, u32[]{:S(2)}) collective-permute-start(f32[256,256]{1,0:T(8,128)} %refs_4_.2), channel_id=1, source_target_pairs={{0,5},{1,4},{2,7},{3,6},{4,1},{5,0},{6,3},{7,2},{8,13},{9,12},{10,... | collective-permute-start | bytes 786440 | tf_op jit(solution)/shard_map/ppermute | solution.py:256
  2.3 18.2 %collective-permute-start.13 = (f32[512,256]{1,0:T(8,128)}, f32[512,256]{1,0:T(8,128)S(1)}, u32[]{:S(2)}, u32[]{:S(2)}) collective-permute-start(f32[512,256]{1,0:T(8,128)} %refs_4_.3), channel_id=1, source_target_pairs={{0,8},{8,0},{16,24},{24,16},{1,9},{9,1},{17,25},{25,17},{2,10},{10... | collective-permute-start | bytes 1572872 | tf_op jit(solution)/shard_map/ppermute | solution.py:256
  2.3 22.7 %collective-permute-start.14 = (f32[512,256]{1,0:T(8,128)}, f32[512,256]{1,0:T(8,128)S(1)}, u32[]{:S(2)}, u32[]{:S(2)}) collective-permute-start(f32[512,256]{1,0:T(8,128)} %refs_4_.3), channel_id=1, source_target_pairs={{8,16},{16,8},{9,17},{17,9},{10,18},{18,10},{11,19},{19,11},{12,20... | collective-permute-start | bytes 1572872 | tf_op jit(solution)/shard_map/ppermute | solution.py:264
  8.2 8.8 %collective-permute-start.6 = (f32[256,256]{1,0:T(8,128)}, f32[256,256]{1,0:T(8,128)S(1)}, u32[]{:S(2)}, u32[]{:S(2)}) collective-permute-start(f32[256,256]{1,0:T(8,128)} %refs_4_.2), channel_id=1, source_target_pairs={{0,2},{1,3},{2,0},{3,1},{4,6},{5,7},{6,4},{7,5},{8,10},{9,11},{10,... | collective-permute-start | bytes 786440 | tf_op jit(solution)/shard_map/ppermute | solution.py:256
  9.4 14.2 %collective-permute-start.7 = (f32[256,256]{1,0:T(8,128)}, f32[256,256]{1,0:T(8,128)S(1)}, u32[]{:S(2)}, u32[]{:S(2)}) collective-permute-start(f32[256,256]{1,0:T(8,128)} %refs_4_.2), channel_id=1, source_target_pairs={{0,3},{1,2},{2,1},{3,0},{4,7},{5,6},{6,5},{7,4},{8,11},{9,10},{10,... | collective-permute-start | bytes 786440 | tf_op jit(solution)/shard_map/ppermute | solution.py:256
  14.8 16.2 %collective-permute-start.8 = (f32[256,256]{1,0:T(8,128)}, f32[256,256]{1,0:T(8,128)S(1)}, u32[]{:S(2)}, u32[]{:S(2)}) collective-permute-start(f32[256,256]{1,0:T(8,128)} %refs_4_.2), channel_id=1, source_target_pairs={{0,6},{1,7},{2,4},{3,5},{4,2},{5,3},{6,0},{7,1},{8,14},{9,15},{10,... | collective-permute-start | bytes 786440 | tf_op jit(solution)/shard_map/ppermute | solution.py:256
  17.0 17.3 %collective-permute-start.9 = (f32[256,256]{1,0:T(8,128)}, f32[256,256]{1,0:T(8,128)S(1)}, u32[]{:S(2)}, u32[]{:S(2)}) collective-permute-start(f32[256,256]{1,0:T(8,128)} %refs_4_.2), channel_id=1, source_target_pairs={{0,7},{1,6},{2,5},{3,4},{4,3},{5,2},{6,1},{7,0},{8,15},{9,14},{10,... | collective-permute-start | bytes 786440 | tf_op jit(solution)/shard_map/ppermute | solution.py:256
  20.5 17.9 %copy-start.6 = (f32[512,256]{1,0:T(8,128)}, f32[512,256]{1,0:T(8,128)S(1)}, u32[]{:S(2)}) copy-start(f32[512,256]{1,0:T(8,128)S(1)} %collective-permute-done.13.refs_5_) | copy-start | bytes 1572868
  20.5 18.0 %collective-permute-start.16 = (f32[512,256]{1,0:T(8,128)S(1)}, f32[512,256]{1,0:T(8,128)S(1)}, u32[]{:S(2)}, u32[]{:S(2)}) collective-permute-start(f32[512,256]{1,0:T(8,128)S(1)} %collective-permute-done.13.refs_5_), channel_id=1, source_target_pairs={{8,16},{16,8},{9,17},{17,9},{10,18},{18,10},{11,19},{19,11},{12,20... | collective-permute-start | bytes 1572872 | tf_op jit(solution)/shard_map/ppermute | solution.py:265
  23.7 20.6 %collective-permute-start.17 = (f32[512,256]{1,0:T(8,128)S(1)}, f32[512,256]{1,0:T(8,128)S(1)}, u32[]{:S(2)}, u32[]{:S(2)}) collective-permute-start(f32[512,256]{1,0:T(8,128)S(1)} %collective-permute-done.13.refs_5_), channel_id=1, source_target_pairs={{16,0},{8,24},{17,1},{9,25},{18,2},{10,26},{19,3},{11,27},{20,4},{... | collective-permute-start | bytes 1572872 | tf_op jit(solution)/shard_map/ppermute | solution.py:267
  25.0 13.4 %copy-start.10 = (f32[512,256]{1,0:T(8,128)}, f32[512,256]{1,0:T(8,128)S(1)}, u32[]{:S(2)}) copy-start(f32[512,256]{1,0:T(8,128)S(1)} %collective-permute-done.14.refs_6_) | copy-start | bytes 1572868
  25.0 23.9 %collective-permute-start.15 = (f32[512,256]{1,0:T(8,128)S(1)}, f32[512,256]{1,0:T(8,128)S(1)}, u32[]{:S(2)}, u32[]{:S(2)}) collective-permute-start(f32[512,256]{1,0:T(8,128)S(1)} %collective-permute-done.14.refs_6_), channel_id=1, source_target_pairs={{8,0},{16,24},{9,1},{17,25},{10,2},{18,26},{11,3},{19,27},{12,4},{... | collective-permute-start | bytes 1572872 | tf_op jit(solution)/shard_map/ppermute | solution.py:266
  31.1 17.9 %copy-start.2 = (s32[4,8]{1,0:T(4,128)S(1)}, s32[4,8]{1,0:T(4,128)}, u32[]{:S(2)}) copy-start(s32[4,8]{1,0:T(4,128)} %refs_2_.3) | copy-start | bytes 388
  38.4 17.6 %copy-start = (f32[256,256]{1,0:T(8,128)S(1)}, f32[256,256]{1,0:T(8,128)}, u32[]{:S(2)}) copy-start(f32[256,256]{1,0:T(8,128)} %refs_4_.2) | copy-start | bytes 786436
  38.4 17.6 %copy-start.1 = (s32[8,4]{0,1:T(4,128)S(1)}, s32[8,4]{0,1:T(4,128)}, u32[]{:S(2)}) copy-start(s32[8,4]{0,1:T(4,128)} %param.18) | copy-start | bytes 388
  56.0 1.4 copy-start.16
  56.0 1.4 copy-start.22
  56.0 1.4 copy-start.28
  56.0 57.0 %collective-permute-start.1 = (f32[512,512]{1,0:T(8,128)S(1)}, f32[512,512]{1,0:T(8,128)}, u32[]{:S(2)}, u32[]{:S(2)}) collective-permute-start(f32[512,512]{1,0:T(8,128)S(1)} %get-tuple-element.154), channel_id=1, source_target_pairs={{0,16},{8,24},{16,0},{24,8},{1,17},{9,25},{17,1},{25,9},{2,18},{10... | collective-permute-start | bytes 3145736 | tf_op jit(solution)/shard_map/cond/branch_1_fun/ppermute | solution.py:256
  57.5 6.4 %copy-start.4 = (f32[512,256]{1,0:T(8,128)S(1)}, f32[512,256]{1,0:T(8,128)}, u32[]{:S(2)}) copy-start(f32[512,256]{1,0:T(8,128)} %get-tuple-element.168.refs_4_) | copy-start | bytes 1572868 | tf_op jit(solution)/shard_map/cond
  57.5 6.4 %copy-start.8 = (f32[512,256]{1,0:T(8,128)S(1)}, f32[512,256]{1,0:T(8,128)}, u32[]{:S(2)}) copy-start(f32[512,256]{1,0:T(8,128)} %get-tuple-element.169.refs_5_) | copy-start | bytes 1572868 | tf_op jit(solution)/shard_map/cond
  57.5 6.4 %copy-start.12 = (f32[512,256]{1,0:T(8,128)S(1)}, f32[512,256]{1,0:T(8,128)}, u32[]{:S(2)}) copy-start(f32[512,256]{1,0:T(8,128)} %get-tuple-element.170.refs_6_) | copy-start | bytes 1572868 | tf_op jit(solution)/shard_map/cond
  57.5 6.4 %copy-start.17 = (f32[512,256]{1,0:T(8,128)S(1)}, f32[512,256]{1,0:T(8,128)}, u32[]{:S(2)}) copy-start(f32[512,256]{1,0:T(8,128)} %copy-done.16) | copy-start | bytes 1572868 | tf_op jit(solution)/shard_map/cond
  57.5 6.5 %copy-start.23 = (f32[512,256]{1,0:T(8,128)S(1)}, f32[512,256]{1,0:T(8,128)}, u32[]{:S(2)}) copy-start(f32[512,256]{1,0:T(8,128)} %copy-done.22) | copy-start | bytes 1572868 | tf_op jit(solution)/shard_map/cond
  57.5 6.5 %copy-start.29 = (f32[512,256]{1,0:T(8,128)S(1)}, f32[512,256]{1,0:T(8,128)}, u32[]{:S(2)}) copy-start(f32[512,256]{1,0:T(8,128)} %copy-done.28) | copy-start | bytes 1572868 | tf_op jit(solution)/shard_map/cond
  114.5 41.6 %collective-permute-start.18 = (f32[512,512]{1,0:T(8,128)S(1)}, f32[512,512]{1,0:T(8,128)S(1)}, u32[]{:S(2)}, u32[]{:S(2)}) collective-permute-start(f32[512,512]{1,0:T(8,128)S(1)} %add.36), channel_id=1, source_target_pairs={{0,2},{1,3},{2,0},{3,1},{4,6},{5,7},{6,4},{7,5},{8,10},{9,11},{10,... | collective-permute-start | bytes 3145736 | tf_op jit(solution)/shard_map/ppermute | solution.py:256
  114.6 46.4 %collective-permute-start.19 = (f32[512,512]{1,0:T(8,128)S(1)}, f32[512,512]{1,0:T(8,128)S(1)}, u32[]{:S(2)}, u32[]{:S(2)}) collective-permute-start(f32[512,512]{1,0:T(8,128)S(1)} %add.36), channel_id=1, source_target_pairs={{0,4},{1,5},{2,6},{3,7},{4,0},{5,1},{6,2},{7,3},{8,12},{9,13},{10,... | collective-permute-start | bytes 3145736 | tf_op jit(solution)/shard_map/ppermute | solution.py:256
  114.7 46.4 %collective-permute-start.20 = (f32[512,512]{1,0:T(8,128)S(1)}, f32[512,512]{1,0:T(8,128)}, u32[]{:S(2)}, u32[]{:S(2)}) collective-permute-start(f32[512,512]{1,0:T(8,128)S(1)} %add.36), channel_id=1, source_target_pairs={{0,6},{1,7},{2,4},{3,5},{4,2},{5,3},{6,0},{7,1},{8,14},{9,15},{10,... | collective-permute-start | bytes 3145736 | tf_op jit(solution)/shard_map/ppermute | solution.py:256
  118.6 37.5 %collective-permute-start.4 = (f32[512,512]{1,0:T(8,128)}, f32[512,512]{1,0:T(8,128)}, u32[]{:S(2)}, u32[]{:S(2)}) collective-permute-start(f32[512,512]{1,0:T(8,128)} %param.4), channel_id=1, source_target_pairs={{0,16},{8,24},{16,0},{24,8},{1,17},{9,25},{17,1},{25,9},{2,18},{10... | collective-permute-start | bytes 3145736 | tf_op jit(solution)/shard_map/cond/branch_1_fun/ppermute | solution.py:256
  162.5 5.5 %collective-permute-start.21 = (f32[512,512]{1,0:T(8,128)}, f32[512,512]{1,0:T(8,128)}, u32[]{:S(2)}, u32[]{:S(2)}) collective-permute-start(f32[512,512]{1,0:T(8,128)} %select_select_fusion), channel_id=1, source_target_pairs={{0,1},{1,0},{2,3},{3,2},{4,5},{5,4},{6,7},{7,6},{8,9},{9,8},{10,11... | collective-permute-start | bytes 3145736 | tf_op jit(solution)/shard_map/ppermute | solution.py:256
